TPU v7x, 32 devices: a whole 2x2x4 slice. The times are simulated.
32 devices in a mesh: dp: 2 (over y), row: 4 (over z), col: 4 (over x, core).
Axes of the slice: x: 2, y: 2, z: 4, core: 2. Of those that a mesh axis runs over, the one named last changes fastest.
Arguments:
- tokens: bfloat16 [2, 16384, 1472], P(None, ('dp', 'row', 'col')), may hold values from -6 to 6
- out_grad: bfloat16 [2, 16384, 1472], P(None, ('dp', 'row', 'col')), may hold values from -6 to 6
- lengths: int32 [2, 32, 2], P(None, ('dp', 'row', 'col')), may hold values from 1 to 384, 512 in all within a row
- offset_bucket: int32 [1023], replicated, may hold values from 0 to 31
- qkv_weight: bfloat16 [1472, 1152], P('dp'), may hold values from -0.078125 to 0.078125
- out_weight: bfloat16 [384, 1472], P(None, 'dp'), may hold values from -1.25 to 1.25
- bias_table: bfloat16 [32, 6], P('dp'), may hold values from -4 to 4
- norm_gains: bfloat16 [2, 1472], P(None, 'dp'), may hold values from 0.5 to 1.5
- inner_weight: bfloat16 [2, 1472, 3584], P(None, ('dp', 'row'), 'col'), may hold values from -0.15625 to 0.15625
- outer_weight: bfloat16 [3584, 1472], P('col', ('dp', 'row')), may hold values from -0.09375 to 0.09375
Outputs:
- layer_out: bfloat16 [2, 16384, 1472], P(None, ('dp', 'row', 'col'))
- tokens_grad: bfloat16 [2, 16384, 1472], P(None, ('dp', 'row', 'col'))
- qkv_grad: float32 [1472, 1152], P('dp')
- out_weight_grad: float32 [384, 1472], P(None, 'dp')
- table_grad: float32 [32, 6], P('dp')
- gains_grad: float32 [2, 1472], P(None, 'dp')
- inner_grad: float32 [2, 1472, 3584], P(None, ('dp', 'row'), 'col')
- outer_grad: float32 [3584, 1472], P('col', ('dp', 'row'))
Inputs may be any that keep to these rules, and one draw needn't show every extreme that they name: Each row holds the lengths of 2 documents that fill one device's 512 tokens of one micro-batch exactly; in each row the longest has at most 384 tokens.
All inputs are finite; a program needn't handle non-finite values.
Results may differ from a plain program's by a relative error of at most 0.029.
Values may be sent and summed in bfloat16 or wider, within the bound.
A program may use at most 152 MiB of HBM per device.

v0:
```python
import jax
import jax.numpy as jnp
from jax import lax
from jax.sharding import PartitionSpec as P

epsilon = 1e-06
masked_score = -1000000000.0
highest = lax.Precision.HIGHEST


def toeplitz(offset_values):
    head_count, span = offset_values.shape
    row_count = (span + 1) // 2
    flipped = offset_values[:, ::-1]
    spread = jnp.broadcast_to(flipped[:, None, :], (head_count, row_count, span)).reshape(
        head_count, row_count * span
    )
    spread = jnp.pad(spread, ((0, 0), (0, row_count))).reshape(
        head_count, row_count, 2 * row_count
    )[:, :, :row_count]
    return spread[:, :, ::-1]


def diagonal_sums(score_grid):
    head_count, row_count, _ = score_grid.shape
    flipped = jnp.pad(score_grid[:, :, ::-1], ((0, 0), (0, 0), (0, row_count)))
    skewed = flipped.reshape(head_count, 2 * row_count * row_count)[
        :, : row_count * (2 * row_count - 1)
    ]
    skewed = skewed.reshape(head_count, row_count, 2 * row_count - 1)
    return jnp.sum(skewed, axis=1)[:, ::-1]


def segment_mask(doc_lengths, row_count):
    places = jnp.arange(row_count, dtype=jnp.int32)
    doc_ends = jnp.cumsum(doc_lengths)
    labels = jnp.sum((places[:, None] >= doc_ends[None, :]).astype(jnp.int32), axis=1)
    return labels[:, None] == labels[None, :]


def rms_normed(values, gain):
    scale = lax.rsqrt(jnp.mean(values * values, axis=1, keepdims=True) + epsilon)
    return values * scale * gain


def gated_unit(gate_in, up_in):
    return jax.nn.gelu(gate_in, approximate=True) * up_in


def attention_scores(queries, key_rows, score_bias, same_doc):
    raw = (
        jnp.einsum("ihd,jhd->hij", queries, key_rows, preferred_element_type=jnp.float32)
        + score_bias
    )
    return jnp.where(same_doc[None], raw, masked_score)


def shards(
    tokens,
    out_grad,
    lengths,
    offset_bucket,
    qkv_weight,
    out_weight,
    bias_table,
    norm_gains,
    inner_weight,
    outer_weight,
):
    micro_count, row_count, model_width = tokens.shape
    head_count = bias_table.shape[1]
    inner_width = out_weight.shape[0]
    head_dim = inner_width // head_count
    bucket_ids = jnp.arange(bias_table.shape[0] * lax.axis_size("dp"), dtype=jnp.int32)
    bucket_onehot = (offset_bucket[:, None] == bucket_ids[None, :]).astype(jnp.float32)
    qkv_acc = jnp.zeros((model_width, 3 * inner_width), jnp.float32)
    out_acc = jnp.zeros((inner_width, model_width), jnp.float32)
    table_acc = jnp.zeros((bucket_ids.shape[0], head_count), jnp.float32)
    gains_acc = jnp.zeros((2, model_width), jnp.float32)
    inner_acc = jnp.zeros((2, model_width, inner_weight.shape[2]), jnp.float32)
    outer_acc = jnp.zeros((outer_weight.shape[0], model_width), jnp.float32)
    outputs = []
    input_grads = []
    for micro_index in range(micro_count):
        qkv_full, out_full, table_full, gains_full = (
            lax.all_gather(qkv_weight, "dp", axis=0, tiled=True),
            lax.all_gather(out_weight, "dp", axis=1, tiled=True),
            lax.all_gather(bias_table, "dp", axis=0, tiled=True),
            lax.all_gather(norm_gains, "dp", axis=1, tiled=True),
        )
        gain_rows = gains_full.astype(jnp.float32)
        same_doc = segment_mask(lengths[micro_index, 0], row_count)
        offset_bias = jnp.dot(bucket_onehot, table_full.astype(jnp.float32), precision=highest)
        score_bias = toeplitz(offset_bias.T)
        tokens_wide = tokens[micro_index].astype(jnp.float32)
        normed_one = rms_normed(tokens_wide, gain_rows[0]).astype(jnp.bfloat16)
        qkv_rows = jnp.dot(normed_one, qkv_full, preferred_element_type=jnp.float32).astype(
            jnp.bfloat16
        )
        queries = qkv_rows[:, :inner_width].reshape(row_count, head_count, head_dim)
        key_rows = qkv_rows[:, inner_width : 2 * inner_width].reshape(
            row_count, head_count, head_dim
        )
        value_rows = qkv_rows[:, 2 * inner_width :].reshape(row_count, head_count, head_dim)
        scores = attention_scores(queries, key_rows, score_bias, same_doc)
        row_peak = jnp.max(scores, axis=2, keepdims=True)
        log_total = row_peak + jnp.log(jnp.sum(jnp.exp(scores - row_peak), axis=2, keepdims=True))
        attn_low = jnp.exp(scores - log_total).astype(jnp.bfloat16)
        attended = jnp.einsum(
            "hij,jhd->ihd", attn_low, value_rows, preferred_element_type=jnp.float32
        )
        attended = attended.reshape(row_count, inner_width).astype(jnp.bfloat16)
        residual = tokens_wide + jnp.dot(attended, out_full, preferred_element_type=jnp.float32)
        normed_two = rms_normed(residual, gain_rows[1]).astype(jnp.bfloat16)
        gathered = lax.all_gather(normed_two, "col", axis=0, tiled=True)
        inner_full, outer_full = (
            lax.all_gather(inner_weight, ("dp", "row"), axis=1, tiled=True),
            lax.all_gather(outer_weight, ("dp", "row"), axis=1, tiled=True),
        )
        gate_pre = jnp.dot(gathered, inner_full[0], preferred_element_type=jnp.float32)
        up_pre = jnp.dot(gathered, inner_full[1], preferred_element_type=jnp.float32)
        hidden = gated_unit(gate_pre, up_pre).astype(jnp.bfloat16)
        partial_out = jnp.dot(hidden, outer_full, preferred_element_type=jnp.float32)
        branch = lax.psum_scatter(
            partial_out.astype(jnp.bfloat16), "col", scatter_dimension=0, tiled=True
        ).astype(jnp.float32)
        outputs.append((residual + branch).astype(jnp.bfloat16))
        inner_back, outer_back = (
            lax.all_gather(inner_weight, ("dp", "row"), axis=1, tiled=True),
            lax.all_gather(outer_weight, ("dp", "row"), axis=1, tiled=True),
        )
        grad_low = out_grad[micro_index]
        grad_rows = lax.all_gather(grad_low, "col", axis=0, tiled=True)
        outer_acc = outer_acc + jnp.einsum(
            "tf,td->fd", hidden, grad_rows, preferred_element_type=jnp.float32
        )
        grad_hidden = jnp.einsum(
            "td,fd->tf", grad_rows, outer_back, preferred_element_type=jnp.float32
        )
        _, pull_gelu = jax.vjp(gated_unit, gate_pre, up_pre)
        grad_gate, grad_up = pull_gelu(grad_hidden)
        grad_gate = grad_gate.astype(jnp.bfloat16)
        grad_up = grad_up.astype(jnp.bfloat16)
        inner_acc = inner_acc + jnp.stack(
            [
                jnp.einsum("td,tf->df", gathered, grad_gate, preferred_element_type=jnp.float32),
                jnp.einsum("td,tf->df", gathered, grad_up, preferred_element_type=jnp.float32),
            ]
        )
        partial_back = jnp.einsum(
            "tf,df->td", grad_gate, inner_back[0], preferred_element_type=jnp.float32
        ) + jnp.einsum("tf,df->td", grad_up, inner_back[1], preferred_element_type=jnp.float32)
        grad_normed_two = lax.psum_scatter(partial_back, "col", scatter_dimension=0, tiled=True)
        _, pull_two = jax.vjp(rms_normed, residual, gain_rows[1])
        grad_res_norm, grad_gain_two = pull_two(grad_normed_two)
        grad_residual = grad_low.astype(jnp.float32) + grad_res_norm
        qkv_back, out_back = (
            lax.all_gather(qkv_weight, "dp", axis=0, tiled=True),
            lax.all_gather(out_weight, "dp", axis=1, tiled=True),
        )
        branch_grad = grad_residual.astype(jnp.bfloat16)
        out_acc = out_acc + jnp.einsum(
            "ti,td->id", attended, branch_grad, preferred_element_type=jnp.float32
        )
        grad_attended = jnp.einsum(
            "td,id->ti", branch_grad, out_back, preferred_element_type=jnp.float32
        )
        grad_attended = grad_attended.astype(jnp.bfloat16).reshape(row_count, head_count, head_dim)
        scores_again = attention_scores(queries, key_rows, score_bias, same_doc)
        attn_probs = jnp.exp(scores_again - log_total)
        grad_probs = jnp.einsum(
            "ihd,jhd->hij", grad_attended, value_rows, preferred_element_type=jnp.float32
        )
        row_delta = jnp.sum(attn_probs * grad_probs, axis=2, keepdims=True)
        grad_scores = (attn_probs * (grad_probs - row_delta)).astype(jnp.bfloat16)
        grad_values = jnp.einsum(
            "hij,ihd->jhd",
            attn_probs.astype(jnp.bfloat16),
            grad_attended,
            preferred_element_type=jnp.float32,
        )
        grad_queries = jnp.einsum(
            "hij,jhd->ihd", grad_scores, key_rows, preferred_element_type=jnp.float32
        )
        grad_keys = jnp.einsum(
            "hij,ihd->jhd", grad_scores, queries, preferred_element_type=jnp.float32
        )
        grad_qkv = jnp.concatenate(
            [
                grad_queries.reshape(row_count, inner_width),
                grad_keys.reshape(row_count, inner_width),
                grad_values.reshape(row_count, inner_width),
            ],
            axis=1,
        ).astype(jnp.bfloat16)
        per_offset = diagonal_sums(grad_scores.astype(jnp.float32))
        table_acc = table_acc + jnp.dot(bucket_onehot.T, per_offset.T, precision=highest)
        qkv_acc = qkv_acc + jnp.einsum(
            "td,tc->dc", normed_one, grad_qkv, preferred_element_type=jnp.float32
        )
        grad_normed_one = jnp.einsum(
            "tc,dc->td", grad_qkv, qkv_back, preferred_element_type=jnp.float32
        )
        _, pull_one = jax.vjp(rms_normed, tokens_wide, gain_rows[0])
        grad_tok_norm, grad_gain_one = pull_one(grad_normed_one)
        input_grads.append((grad_residual + grad_tok_norm).astype(jnp.bfloat16))
        gains_acc = gains_acc + jnp.stack([grad_gain_one, grad_gain_two])
    qkv_part, out_part, table_part, gains_part = (
        lax.psum_scatter(
            qkv_acc.astype(jnp.bfloat16), "dp", scatter_dimension=0, tiled=True
        ).astype(jnp.float32),
        lax.psum_scatter(
            out_acc.astype(jnp.bfloat16), "dp", scatter_dimension=1, tiled=True
        ).astype(jnp.float32),
        lax.psum_scatter(
            table_acc.astype(jnp.bfloat16), "dp", scatter_dimension=0, tiled=True
        ).astype(jnp.float32),
        lax.psum_scatter(
            gains_acc.astype(jnp.bfloat16), "dp", scatter_dimension=1, tiled=True
        ).astype(jnp.float32),
    )
    qkv_grad, out_weight_grad, table_grad, gains_grad = (
        lax.psum(qkv_part.astype(jnp.bfloat16), ("row", "col")).astype(jnp.float32),
        lax.psum(out_part.astype(jnp.bfloat16), ("row", "col")).astype(jnp.float32),
        lax.psum(table_part.astype(jnp.bfloat16), ("row", "col")).astype(jnp.float32),
        lax.psum(gains_part.astype(jnp.bfloat16), ("row", "col")).astype(jnp.float32),
    )
    inner_grad, outer_grad = (
        lax.psum_scatter(inner_acc, ("dp", "row"), scatter_dimension=1, tiled=True),
        lax.psum_scatter(outer_acc, ("dp", "row"), scatter_dimension=1, tiled=True),
    )
    return (
        jnp.stack(outputs),
        jnp.stack(input_grads),
        qkv_grad,
        out_weight_grad,
        table_grad,
        gains_grad,
        inner_grad,
        outer_grad,
    )


def solution(mesh):
    return jax.shard_map(
        shards,
        mesh=mesh,
        in_specs=(
            P(None, ("dp", "row", "col"), None),
            P(None, ("dp", "row", "col"), None),
            P(None, ("dp", "row", "col"), None),
            P(),
            P("dp", None),
            P(None, "dp"),
            P("dp", None),
            P(None, "dp"),
            P(None, ("dp", "row"), "col"),
            P("col", ("dp", "row")),
        ),
        out_specs=(
            P(None, ("dp", "row", "col"), None),
            P(None, ("dp", "row", "col"), None),
            P("dp", None),
            P(None, "dp"),
            P("dp", None),
            P(None, "dp"),
            P(None, ("dp", "row"), "col"),
            P("col", ("dp", "row")),
        ),
        check_vma=False,
    )
```

profile of v0, /device:TPU:0, one launch (start us, length us, event | category | flops | bytes accessed | tf_op | source)
XLA Modules:
  0.0 1545.6 jit_solution(15144630438490581380)
XLA Ops:
  66.8 18.1 %copy.114 = f32[1,6,512,1024]{3,2,1,0:T(8,128)} copy(f32[1,6,512,1024]{3,1,2,0:T(8,128)} %bitcast.199) | data formatting | bytes 25165824
  98.5 48.8 %rev.21 = f32[6,512,512]{1,2,0:T(8,128)} reverse(f32[6,512,512]{1,2,0:T(8,128)} %copy.107), dimensions={2} | reverse | bytes 12582912 | tf_op jit(solution)/shard_map/rev | solution.py:21
  172.6 45.1 %all-gather.17.cloned.1.call-done = bf16[2048,1472]{0,1:T(8,128)(2,1)} async-done(((bf16[512,1472]{0,1:T(8,128)(2,1)}), bf16[2048,1472]{0,1:T(8,128)(2,1)}) %all-gather.17.cloned.1.call-update) | async-done | bytes 6029328 | tf_op jit(solution)/shard_map/all_gather | solution.py:115
  238.4 36.2 %all-gather.21.cloned.1.call-done = bf16[896,1472]{0,1:T(8,128)(2,1)} async-done(((bf16[896,184]{0,1:T(8,128)(2,1)}), bf16[896,1472]{0,1:T(8,128)(2,1)}) %all-gather.21.cloned.1.call-update) | async-done | bytes 2637840 | tf_op jit(solution)/shard_map/all_gather | solution.py:118
  274.6 45.5 %all-gather.25.cloned.1.call-done = bf16[1,2048,1472]{1,2,0:T(8,128)(2,1)} async-done(((bf16[1,512,1472]{1,2,0:T(8,128)(2,1)}), bf16[1,2048,1472]{1,2,0:T(8,128)(2,1)}) %all-gather.25.cloned.1.call-update) | async-done | bytes 6029328 | tf_op jit(solution)/shard_map/all_gather | solution.py:133
  320.1 20.3 %multiply_convert_fusion.1 = (bf16[2048,896]{1,0:T(8,128)(2,1)S(1)}, bf16[2048,896]{1,0:T(8,128)(2,1)}, bf16[2048,896]{1,0:T(8,128)(2,1)}) fusion(f32[2048,896]{1,0:T(8,128)} %fusion.50, f32[2048,896]{1,0:T(8,128)} %fusion.52, bf16[896,1472]{0,1:T(8,128)(2,1)} %all-gather.21.cloned.1.call-done, bf16[1,2048,1472]{1,2,0:T(8,128)(2,1)} %all-gather.25.cloned.1.call-done), kind=kOutput, calls=%fused_computation.29 | convolution fusion | flops 5449973760 | bytes 34357248 | tf_op jit(solution)/shard_map/td,fd->tf/dot_general | solution.py:137
  351.2 23.5 %convolution_add_fusion.2 = f32[2048,1472]{0,1:T(8,128)} fusion(f32[2048,1472]{0,1:T(8,128)S(1)} %fusion.48, bf16[2048,896]{1,0:T(8,128)(2,1)S(1)} %get-tuple-element.26, bf16[2,1472,896]{2,1,0:T(8,128)(2,1)} %all-gather.19.cloned.1.call-done), kind=kOutput, calls=%fused_computation.10 | convolution fusion | flops 5405278208 | bytes 30425088 | tf_op jit(solution)/shard_map/tf,df->td/dot_general | solution.py:152
  399.5 71.0 %reduce-scatter.21.cloned.1.call-done = f32[512,1472]{0,1:T(8,128)} async-done(((f32[2048,1472]{0,1:T(8,128)}), f32[512,1472]{0,1:T(8,128)}) %reduce-scatter.21.cloned.1.call-update) | async-done | bytes 3014672 | tf_op jit(solution)/shard_map/reduce_scatter | solution.py:153
  476.8 44.3 %all-gather.23.cloned.1.call-done = bf16[2048,1472]{0,1:T(8,128)(2,1)} async-done(((bf16[512,1472]{0,1:T(8,128)(2,1)}), bf16[2048,1472]{0,1:T(8,128)(2,1)}) %all-gather.23.cloned.1.call-update) | async-done | bytes 6029328 | tf_op jit(solution)/shard_map/all_gather | solution.py:115
  543.9 24.2 %all-gather.27.cloned.1.call-done = bf16[1,2048,1472]{1,2,0:T(8,128)(2,1)} async-done(((bf16[1,512,1472]{1,2,0:T(8,128)(2,1)}), bf16[1,2048,1472]{1,2,0:T(8,128)(2,1)}) %all-gather.27.cloned.1.call-update) | async-done | bytes 6029328 | tf_op jit(solution)/shard_map/all_gather | solution.py:133
  568.1 20.2 %multiply_convert_fusion = (bf16[2048,896]{1,0:T(8,128)(2,1)S(1)}, bf16[2048,896]{1,0:T(8,128)(2,1)}, bf16[2048,896]{1,0:T(8,128)(2,1)}) fusion(f32[2048,896]{1,0:T(8,128)} %fusion.49, f32[2048,896]{1,0:T(8,128)} %fusion.51, bf16[896,1472]{0,1:T(8,128)(2,1)} %all-gather.21.cloned.1.call-done, bf16[1,2048,1472]{1,2,0:T(8,128)(2,1)} %all-gather.27.cloned.1.call-done), kind=kOutput, calls=%fused_computation.28 | convolution fusion | flops 5449973760 | bytes 34357248 | tf_op jit(solution)/shard_map/td,fd->tf/dot_general | solution.py:137
  634.7 72.1 %reduce-scatter.23.cloned.1.call-done = f32[512,1472]{0,1:T(8,128)} async-done(((f32[2048,1472]{0,1:T(8,128)}), f32[512,1472]{0,1:T(8,128)}) %reduce-scatter.23.cloned.1.call-update) | async-done | bytes 3014672 | tf_op jit(solution)/shard_map/reduce_scatter | solution.py:153
  710.9 55.0 %reduce-scatter.17.cloned.1.call-done = bf16[512,1472]{0,1:T(8,128)(2,1)} async-done(((bf16[2048,1472]{0,1:T(8,128)(2,1)}), bf16[512,1472]{0,1:T(8,128)(2,1)}) %reduce-scatter.17.cloned.1.call-update) | async-done | bytes 1507344 | tf_op jit(solution)/shard_map/reduce_scatter | solution.py:124
  766.0 59.2 %reduce-scatter.19.cloned.1.call-done = bf16[512,1472]{0,1:T(8,128)(2,1)} async-done(((bf16[2048,1472]{0,1:T(8,128)(2,1)}), bf16[512,1472]{0,1:T(8,128)(2,1)}) %reduce-scatter.19.cloned.1.call-update) | async-done | bytes 1507344 | tf_op jit(solution)/shard_map/reduce_scatter | solution.py:124
  877.3 31.5 %rev.24 = f32[6,512,512]{1,2,0:T(8,128)} reverse(bf16[6,512,512]{1,2,0:T(8,128)(2,1)S(1)} %multiply_convert_fusion.4), dimensions={2} | reverse | bytes 9437184 | tf_op jit(solution)/shard_map/rev | solution.py:26
  908.8 45.9 %rev.22 = f32[6,512,512]{1,2,0:T(8,128)} reverse(bf16[6,512,512]{1,2,0:T(8,128)(2,1)} %copy-done.2), dimensions={2} | reverse | bytes 9437184 | tf_op jit(solution)/shard_map/rev | solution.py:26
  987.3 18.0 %copy.111 = f32[1,6,512,1024]{3,1,2,0:T(8,128)} copy(f32[1,6,512,1024]{3,2,1,0:T(8,128)} %pad_bitcast_fusion.1) | data formatting | bytes 25165824
  1029.0 14.2 reshape.323
  1058.5 18.0 %copy.112 = f32[1,6,512,1024]{3,1,2,0:T(8,128)} copy(f32[1,6,512,1024]{3,2,1,0:T(8,128)} %pad_bitcast_fusion) | data formatting | bytes 25165824
  1100.1 14.4 reshape.325
  1195.3 33.1 %all-reduce.4 = (bf16[16,6]{0,1:T(8,128)(2,1)S(1)}, bf16[2,736]{1,0:T(2,128)(2,1)S(1)}) all-reduce(bf16[16,6]{0,1:T(8,128)(2,1)S(1)} %copy.104, bf16[2,736]{1,0:T(2,128)(2,1)S(1)} %copy.106), channel_id=1, replica_groups=mesh['dp'=2,'row'=4,'col'=4] {'row','col'}, use_global_device_ids=true, to_apply=%region_29.30 | all-reduce | flops 1568 | bytes 6272 | tf_op jit(solution)/shard_map/psum | solution.py:225
  1229.6 20.1 %all-reduce.8.cloned.1.call-done = (bf16[736,1152]{1,0:T(8,128)(2,1)}, bf16[384,736]{0,1:T(8,128)(2,1)}) async-done(((bf16[736,1152]{1,0:T(8,128)(2,1)}, bf16[384,736]{0,1:T(8,128)(2,1)}), (bf16[736,1152]{1,0:T(8,128)(2,1)}, bf16[384,736]{0,1:T(8,128)(2,1)})) %all-reduce.8.cloned.1.call-update) | async-done | bytes 2261008 | tf_op jit(solution)/shard_map/psum | solution.py:223
  1255.2 100.5 %reduce-scatter.35.cloned.1.call-done = f32[896,184]{0,1:T(8,128)} async-done(((f32[896,1472]{0,1:T(8,128)}), f32[896,184]{0,1:T(8,128)}) %reduce-scatter.35.cloned.1.call-update) | async-done | bytes 659472
  1355.7 183.2 %reduce-scatter.29.cloned.1.call-done = f32[2,184,896]{2,1,0:T(8,128)} async-done(((f32[2,1472,896]{2,1,0:T(8,128)}), f32[2,184,896]{2,1,0:T(8,128)}) %reduce-scatter.29.cloned.1.call-update) | async-done | bytes 1318928 | tf_op jit(solution)/shard_map/reduce_scatter | solution.py:229
  (339 shorter events, 468.0 us)
Async XLA Ops:
  7.2 141.4 %all-gather.13.cloned.1.call-start = ((), (), s32[]{:S(2)}) async-start(), calls=%async_computation.10 | async-start | bytes 5087232 | tf_op jit(solution)/shard_map/all_gather | solution.py:86
  7.9 154.0 %all-gather.15.cloned.1.call-start = ((), (), s32[]{:S(2)}) async-start(), calls=%async_computation.11 | async-start | bytes 1695744 | tf_op jit(solution)/shard_map/all_gather | solution.py:87
  8.7 164.0 %all-gather.19.cloned.1.call-start = ((), (), s32[]{:S(2)}) async-start(), calls=%async_computation.13 | async-start | bytes 5935104 | tf_op jit(solution)/shard_map/all_gather | solution.py:117
  9.4 208.4 %all-gather.17.cloned.1.call-start = ((), (), s32[]{:S(2)}) async-start(), calls=%async_computation.12 | async-start | bytes 7536640 | tf_op jit(solution)/shard_map/all_gather | solution.py:115
  98.5 48.8 %copy-start.66 = (s32[2,1,2]{2,1,0:T(1,128)S(1)}, s32[2,1,2]{2,1,0:T(1,128)}, u32[]{:S(2)}) copy-start(s32[2,1,2]{2,1,0:T(1,128)} %param.12) | copy-start | bytes 52
  98.5 49.1 %copy-start.7 = (bf16[2,512,1472]{1,2,0:T(8,128)(2,1)S(1)}, bf16[2,512,1472]{1,2,0:T(8,128)(2,1)}, u32[]{:S(2)}) copy-start(bf16[2,512,1472]{1,2,0:T(8,128)(2,1)} %param.10) | copy-start | bytes 9043972
  147.6 228.4 %copy-start.44 = (f32[1472]{0:T(1024)}, f32[1472]{0:T(1024)S(1)}, u32[]{:S(2)}) copy-start(f32[1472]{0:T(1024)S(1)} %get-tuple-element.21) | copy-start | bytes 17668
  148.3 226.8 %copy-start.54 = (f32[512]{0:T(512)}, f32[512]{0:T(512)S(1)}, u32[]{:S(2)}) copy-start(f32[512]{0:T(512)S(1)} %get-tuple-element.19) | copy-start | bytes 6148
  166.3 108.3 %all-gather.21.cloned.1.call-start = ((), (), s32[]{:S(2)}) async-start(), calls=%async_computation.14 | async-start | bytes 2967552 | tf_op jit(solution)/shard_map/all_gather | solution.py:118
  166.9 153.2 %all-gather.25.cloned.1.call-start = ((), (), s32[]{:S(2)}) async-start(), calls=%async_computation.23 | async-start | bytes 7536640 | tf_op jit(solution)/shard_map/all_gather | solution.py:133
  170.6 299.9 %reduce-scatter.21.cloned.1.call-start = ((), (), s32[]{:S(2)}) async-start(), calls=%async_computation.18 | async-start | bytes 15073280 | tf_op jit(solution)/shard_map/reduce_scatter | solution.py:153
  374.7 146.3 %all-gather.23.cloned.1.call-start = ((), (), s32[]{:S(2)}) async-start(), calls=%async_computation.16 | async-start | bytes 7536640 | tf_op jit(solution)/shard_map/all_gather | solution.py:115
  392.8 449.4 %copy-start.32 = (f32[6,512]{1,0:T(8,128)}, f32[6,512]{1,0:T(8,128)S(1)}, u32[]{:S(2)}) copy-start(f32[6,512]{1,0:T(8,128)S(1)} %log_add_fusion) | copy-start | bytes 36868
  476.0 92.1 %all-gather.27.cloned.1.call-start = ((), (), s32[]{:S(2)}) async-start(), calls=%async_computation.24 | async-start | bytes 7536640 | tf_op jit(solution)/shard_map/all_gather | solution.py:133
  476.7 230.0 %reduce-scatter.23.cloned.1.call-start = ((), (), s32[]{:S(2)}) async-start(), calls=%async_computation.19 | async-start | bytes 15073280 | tf_op jit(solution)/shard_map/reduce_scatter | solution.py:153
  611.0 155.0 %reduce-scatter.17.cloned.1.call-start = ((), (), s32[]{:S(2)}) async-start(), calls=%async_computation.15 | async-start | bytes 7536640 | tf_op jit(solution)/shard_map/reduce_scatter | solution.py:124
  622.0 203.1 %reduce-scatter.19.cloned.1.call-start = ((), (), s32[]{:S(2)}) async-start(), calls=%async_computation.17 | async-start | bytes 7536640 | tf_op jit(solution)/shard_map/reduce_scatter | solution.py:124
  634.0 500.3 %reduce-scatter.27.cloned.1.call-start = ((), (), s32[]{:S(2)}) async-start(), calls=%async_computation.21 | async-start | bytes 1695744 | tf_op jit(solution)/shard_map/reduce_scatter | solution.py:212
  853.1 281.2 %reduce-scatter.25.cloned.1.call-start = ((), (), s32[]{:S(2)}) async-start(), calls=%async_computation.20 | async-start | bytes 5087232 | tf_op jit(solution)/shard_map/reduce_scatter | solution.py:209
  876.6 316.9 %reduce-scatter.31.cloned.1.call-start = ((), (), s32[]{:S(2)}) async-start(), calls=%async_computation.25 | async-start | bytes 12288
  1122.2 72.1 %reduce-scatter.33.cloned.1.call-start = ((), (), s32[]{:S(2)}) async-start(), calls=%async_computation.26 | async-start | bytes 565248
  1123.3 126.4 %all-reduce.8.cloned.1.call-start = ((), (), s32[]{:S(2)}) async-start(), calls=%async_computation.28 | async-start | bytes 4521984 | tf_op jit(solution)/shard_map/psum | solution.py:223
  1134.3 221.4 %reduce-scatter.35.cloned.1.call-start = ((), (), s32[]{:S(2)}) async-start(), calls=%async_computation.27 | async-start | bytes 5935104
  1146.2 392.7 %reduce-scatter.29.cloned.1.call-start = ((), (), s32[]{:S(2)}) async-start(), calls=%async_computation.22 | async-start | bytes 11870208 | tf_op jit(solution)/shard_map/reduce_scatter | solution.py:229
  (80 other events, 441.8 us)
Sparse Core Ops, SparseCore 0:
  9.5 50.3 all-gather.12
  61.5 22.2 all-gather.14
  85.9 86.6 all-gather.18
  174.6 43.0 all-gather.16
  219.7 54.8 all-gather.20
  276.6 43.4 all-gather.24
  374.8 95.6 reduce-scatter.20
  476.1 44.8 all-gather.22
  523.2 44.8 all-gather.26
  611.1 95.6 reduce-scatter.22
  709.3 56.6 reduce-scatter.16
  768.5 56.5 reduce-scatter.18
  853.3 21.1 reduce-scatter.26
  877.2 46.0 reduce-scatter.24
  1122.3 9.7 reduce-scatter.30
  1134.2 12.9 reduce-scatter.32
  1150.6 99.0 all-reduce.7
  1253.6 102.0 reduce-scatter.34
  1360.1 178.7 reduce-scatter.28
where the time goes:
time: 1560 us; the launch traced here: 1550 us
  waiting for transfers between devices  762 us (49%)
  local copies, waits for them, and re-layouts  372 us (24%)
  matrix products  291 us (19%)
  other arithmetic  61.7 us (4%)
  blocking collectives  43 us (3%)
    reduce_scatter x1, waiting for transfers between devices, shards(): lax.psum_scatter(inner_acc, ('dp', 'row'), scatter_dimension=1, tiled=True)  183 us
    unnamed x190, local copies, waits for them, and re-layouts  146 us
    reduce_scatter x2, waiting for transfers between devices, shards(): lax.psum_scatter(partial_back, 'col', scatter_dimension=0, tiled=True)  143 us
    reduce_scatter x2, waiting for transfers between devices, shards(): lax.psum_scatter(partial_out.astype(jnp.bfloat16), 'col', scatter_dimensi...  114 us
    unnamed x22, waiting for transfers between devices  104 us
    all_gather x2, waiting for transfers between devices, shards(): gathered = lax.all_gather(normed_two, 'col', axis=0, tiled=True)  89.4 us
    rev x2, local copies, waits for them, and re-layouts, diagonal_sums(): flipped = jnp.pad(score_grid[:, :, ::-1], ((0, 0), (0, 0), (0, row_count)))  77.3 us
    all_gather x2, waiting for transfers between devices, shards(): grad_rows = lax.all_gather(grad_low, 'col', axis=0, tiled=True)  69.7 us
  transfers between devices with their start and end apart: 19, of which 13 were waited for; matrix products, arithmetic and copies ran while one was open for 38% of the time, Pallas kernels for 0%

commit v1 on v0

v1 whole, which is shorter than its diff:
```python
import functools

import jax
import jax.numpy as jnp
from jax import lax
from jax.experimental import pallas as pl
from jax.experimental.pallas import tpu as pltpu
from jax.sharding import PartitionSpec as P

epsilon = 1e-06
masked_score = -1000000000.0
highest = lax.Precision.HIGHEST
gelu_scale = 0.7978845608028654
gelu_cubic = 0.044715
MESH = pl.DeviceIdType.MESH
f32 = jnp.float32
bf16 = jnp.bfloat16
tile = 128
vmem_bytes = 63 * 1024 * 1024


def dot_nn(a, b):
    return lax.dot_general(a, b, (((1,), (0,)), ((), ())), preferred_element_type=f32)


def dot_nt(a, b):
    return lax.dot_general(a, b, (((1,), (1,)), ((), ())), preferred_element_type=f32)


def dot_tn(a, b):
    return lax.dot_general(a, b, (((0,), (0,)), ((), ())), preferred_element_type=f32)


def bucket_onehot(bucket_ref, bucket_count):
    span = bucket_ref.shape[1]
    ids = lax.broadcasted_iota(jnp.int32, (bucket_count, span), 0)
    return ids == jnp.broadcast_to(bucket_ref[0:1, :], (bucket_count, span))


def fill_bias_tiles(tables, bucket_ref, tiles_ref):
    head_count, diag_count = tiles_ref.shape[:2]
    bucket_count = sum(table.shape[1] for table in tables)
    onehot = bucket_onehot(bucket_ref, bucket_count).astype(f32)
    rev = None
    start = 0
    for table in tables:
        stop = start + table.shape[1]
        part = dot_nn(table, onehot[start:stop].astype(bf16))
        rev = part if rev is None else rev + part
        start = stop
    for h in range(head_count):
        for d in range(diag_count):
            row = rev[h : h + 1, tile * d : tile * d + 2 * tile]
            wide = jnp.broadcast_to(row, (tile, 2 * tile))
            turned = pltpu.roll(wide, tile + 1, 1, stride=1, stride_axis=0)[:, :tile]
            tiles_ref[h, d] = turned.astype(tiles_ref.dtype)


def bias_block(tiles_ref, h, key_block, blocks):
    return jnp.concatenate(
        [tiles_ref[h, q - key_block + blocks - 1] for q in range(blocks)], axis=1
    )


def doc_labels(lens_ref, axis, rows):
    shape = (rows, 1) if axis == 0 else (1, rows)
    place = lax.broadcasted_iota(jnp.int32, shape, axis)
    label = jnp.zeros(shape, jnp.int32)
    end = jnp.int32(0)
    for slot in range(lens_ref.shape[2]):
        end = end + lens_ref[0, 0, slot]
        label = label + (place >= end).astype(jnp.int32)
    return label


def masked_scores(key_rows, query_cols, tiles_ref, h, same_doc, blocks):
    raw = dot_nn(key_rows, query_cols)
    bias = jnp.concatenate([bias_block(tiles_ref, h, kb, blocks) for kb in range(blocks)], axis=0)
    return jnp.where(same_doc, raw + bias.astype(f32), masked_score)


def pad_cotangent(og_ref, og_pad_ref, og_pad_t_ref, shard_rows, pad_rows):
    model, rows = og_ref.shape[1:]
    for k in range(model // shard_rows):
        part = slice(k * shard_rows, (k + 1) * shard_rows)
        og_pad_t_ref[k * pad_rows : k * pad_rows + shard_rows, :] = (
            og_ref[0, part, :].astype(f32).astype(bf16)
        )
        rest = slice(k * pad_rows + shard_rows, (k + 1) * pad_rows)
        if pad_rows > shard_rows:
            og_pad_t_ref[rest, :] = jnp.zeros((pad_rows - shard_rows, rows), bf16)
    og_pad_ref[...] = og_pad_t_ref[...].T


def attend(
    lens_ref,
    tok_ref,
    qkv_w_ref,
    out_w_ref,
    gains_ref,
    normed_ref,
    normed_t_ref,
    qkv_ref,
    attended_ref,
    log_ref,
    residual_ref,
    tiles_ref,
    scaled_ref,
    shard_rows,
    pad_rows,
    between,
):
    model, rows = tok_ref.shape[1:]
    inner = attended_ref.shape[1]
    head_count = tiles_ref.shape[0]
    head_dim = inner // head_count
    blocks = rows // tile
    parts = model // shard_rows
    slabs, slab_rows = qkv_w_ref.shape[:2]

    square = jnp.zeros((1, rows), f32)
    for k in range(parts):
        x = tok_ref[0, k * shard_rows : (k + 1) * shard_rows, :].astype(f32)
        square = square + jnp.sum(x * x, axis=0, keepdims=True)
    scale = lax.rsqrt(square / model + epsilon)
    for k in range(parts):
        part = slice(k * shard_rows, (k + 1) * shard_rows)
        x = tok_ref[0, part, :].astype(f32)
        scaled_ref[part, :] = x * scale * gains_ref[part, 0:1]
    total = None
    for slab in range(slabs):
        normed = scaled_ref[slab * slab_rows : (slab + 1) * slab_rows, :].astype(bf16)
        product = dot_tn(qkv_w_ref[slab], normed)
        total = product if total is None else total + product
    qkv_ref[0] = total.astype(bf16)

    same_doc = doc_labels(lens_ref, 0, rows) == doc_labels(lens_ref, 1, rows)

    def head(h, carry):
        base = pl.multiple_of(h * head_dim, head_dim)
        query_cols = qkv_ref[0, pl.ds(base, head_dim), :]
        key_cols = qkv_ref[0, pl.ds(inner + base, head_dim), :]
        value_cols = qkv_ref[0, pl.ds(2 * inner + base, head_dim), :]
        scores = masked_scores(key_cols.T, query_cols, tiles_ref, h, same_doc, blocks)
        peak = jnp.max(scores, axis=0, keepdims=True)
        weight = jnp.exp(scores - peak)
        total = jnp.sum(weight, axis=0, keepdims=True)
        low = (weight * (1.0 / total)).astype(bf16)
        attended_ref[0, pl.ds(base, head_dim), :] = dot_nn(value_cols, low).astype(bf16)
        log_ref[0, h] = jnp.broadcast_to(peak + jnp.log(total), (8, rows))
        return carry

    lax.fori_loop(0, head_count, head, 0)
    between()

    for slab in range(slabs):
        scaled_ref[slab * slab_rows : (slab + 1) * slab_rows, :] = dot_nn(
            out_w_ref[slab], attended_ref[0]
        )
    square = jnp.zeros((1, rows), f32)
    for k in range(parts):
        part = slice(k * shard_rows, (k + 1) * shard_rows)
        x = scaled_ref[part, :] + tok_ref[0, part, :].astype(f32)
        residual_ref[k * pad_rows : k * pad_rows + shard_rows, :] = x
        square = square + jnp.sum(x * x, axis=0, keepdims=True)
    scale = lax.rsqrt(square / model + epsilon)
    for k in range(parts):
        part = slice(k * shard_rows, (k + 1) * shard_rows)
        dest = slice(k * pad_rows, k * pad_rows + shard_rows)
        rest = slice(k * pad_rows + shard_rows, (k + 1) * pad_rows)
        x = residual_ref[dest, :]
        normed_t_ref[dest, :] = (x * scale * gains_ref[part, 1:2]).astype(bf16)
        if pad_rows > shard_rows:
            normed_t_ref[rest, :] = jnp.zeros((pad_rows - shard_rows, rows), bf16)
            residual_ref[rest, :] = jnp.zeros((pad_rows - shard_rows, rows), f32)
    normed_ref[...] = normed_t_ref[...].T


def attention_forward_kernel(
    lens_ref,
    tok_ref,
    og_ref,
    qkv_w_ref,
    out_w_ref,
    gains_ref,
    table_ref,
    bucket_ref,
    normed_ref,
    normed_t_ref,
    og_pad_ref,
    og_pad_t_ref,
    qkv_ref,
    attended_ref,
    log_ref,
    residual_ref,
    tiles_ref,
    scaled_ref,
    *,
    shard_rows,
    pad_rows,
):
    @pl.when(pl.program_id(0) == 0)
    def _():
        fill_bias_tiles([table_ref[...]], bucket_ref, tiles_ref)

    pad_cotangent(og_ref, og_pad_ref, og_pad_t_ref, shard_rows, pad_rows)
    attend(
        lens_ref, tok_ref, qkv_w_ref, out_w_ref, gains_ref, normed_ref, normed_t_ref, qkv_ref,
        attended_ref, log_ref, residual_ref, tiles_ref, scaled_ref, shard_rows, pad_rows,
        lambda: None,
    )


def forward_outputs(micro, heads, inner, model, rows, wide):
    once = lambda shape: pl.BlockSpec((1,) + shape, lambda m: (m,) + (0,) * len(shape))
    tokens = micro * rows
    across = pl.BlockSpec((rows, wide), lambda m: (m, 0))
    along = pl.BlockSpec((wide, rows), lambda m: (0, m))
    specs = [
        across, along, across, along, once((3 * inner, rows)), once((inner, rows)),
        once((heads, 8, rows)), along,
    ]
    shapes = [
        jax.ShapeDtypeStruct((tokens, wide), bf16),
        jax.ShapeDtypeStruct((wide, tokens), bf16),
        jax.ShapeDtypeStruct((tokens, wide), bf16),
        jax.ShapeDtypeStruct((wide, tokens), bf16),
        jax.ShapeDtypeStruct((micro, 3 * inner, rows), bf16),
        jax.ShapeDtypeStruct((micro, inner, rows), bf16),
        jax.ShapeDtypeStruct((micro, heads, 8, rows), f32),
        jax.ShapeDtypeStruct((wide, tokens), f32),
    ]
    return specs, shapes


def attention_forward(
    lens, tok, og, qkv_w, out_w, gains, table, bucket, heads, shard_rows, pad_rows
):
    micro, model, rows = tok.shape
    inner = out_w.shape[2]
    wide = model // shard_rows * pad_rows
    whole = pl.BlockSpec(memory_space=pltpu.VMEM)
    once = lambda shape: pl.BlockSpec((1,) + shape, lambda m: (m,) + (0,) * len(shape))
    out_specs, out_shape = forward_outputs(micro, heads, inner, model, rows, wide)
    return pl.pallas_call(
        functools.partial(attention_forward_kernel, shard_rows=shard_rows, pad_rows=pad_rows),
        grid=(micro,),
        in_specs=[
            pl.BlockSpec((1, 1, lens.shape[2]), lambda m: (m, 0, 0), memory_space=pltpu.SMEM),
            once((model, rows)),
            once((model, rows)),
            whole,
            whole,
            whole,
            whole,
            whole,
        ],
        out_specs=out_specs,
        out_shape=out_shape,
        scratch_shapes=[
            pltpu.VMEM((heads, 2 * (rows // tile) - 1, tile, tile), bf16),
            pltpu.VMEM((model, rows), f32),
        ],
        compiler_params=pltpu.CompilerParams(vmem_limit_bytes=vmem_bytes),
        name="attention_forward",
    )(lens, tok, og, qkv_w, out_w, gains, table, bucket)


class Hidden:
    block = 256
    span = 512

    def __init__(
        self, matrices, normed, normed_t, og, og_t, branch, back, hidden, gate, up, grad_of
    ):
        self.matrices = matrices
        self.normed, self.normed_t, self.og, self.og_t = normed, normed_t, og, og_t
        self.branch, self.back = branch, back
        self.hidden, self.gate, self.up = hidden, gate, up
        self.grad_of = grad_of

    def matrix(self, which, rows=slice(None)):
        return jnp.concatenate([part[rows, :] for part in self.matrices[which]], axis=1)

    def project(self, start, stop):
        def step(b, carry):
            rows = pl.ds(pl.multiple_of(b * self.block, self.block), self.block)
            gate = dot_nn(self.normed[rows, :], self.matrix(0))
            up = dot_nn(self.normed[rows, :], self.matrix(1))
            grad = dot_nn(self.og[rows, :], self.matrix(2))
            cube = gelu_cubic * gate * gate
            t = jnp.tanh(gelu_scale * gate * (1.0 + cube))
            half = 0.5 * (1.0 + t)
            act = gate * half
            slope = half + (0.5 * gelu_scale) * gate * (1.0 - t * t) * (1.0 + 3.0 * cube)
            self.hidden[rows, :] = (act * up).astype(bf16)
            self.gate[rows, :] = (grad * up * slope).astype(bf16)
            self.up[rows, :] = (grad * act).astype(bf16)
            return carry

        lax.fori_loop(start, stop, step, 0)

    def weights(self, start, stop):
        tokens = self.normed.shape[0]
        span = self.span

        def step(b, carry):
            rows = pl.ds(pl.multiple_of(b * span, span), span)
            for which, (left, right) in enumerate(
                (
                    (self.normed_t, self.gate),
                    (self.normed_t, self.up),
                    (self.og_t, self.hidden),
                )
            ):
                grad = dot_nn(left[rows, :], right[...]).astype(bf16)
                for j in range(len(self.matrices[which])):
                    self.grad_of(which, j)[rows, :] = grad[:, j * tile : (j + 1) * tile]
            for which, parts, into in (
                (2, (self.hidden,), self.branch),
                (0, (self.gate, self.up), self.back),
            ):
                for half in range(tokens // span):
                    cols = slice(half * span, (half + 1) * span)
                    total = into[rows, cols]
                    for offset, part in enumerate(parts):
                        total = total + dot_nt(self.matrix(which + offset, rows), part[cols, :])
                    into[rows, cols] = total
            return carry

        lax.fori_loop(start, stop, step, 0)


def feed_forward_kernel(
    normed_hbm,
    normed_t_hbm,
    og_hbm,
    og_t_hbm,
    residual_hbm,
    weight_ref,
    layer_ref,
    back_hbm,
    grad_ref,
    normed_ref,
    normed_t_ref,
    og_ref,
    og_t_ref,
    branch_ref,
    back_ref,
    hidden_ref,
    gate_ref,
    up_ref,
    sems,
    *,
    shard_rows,
    pad_rows,
):
    step = pl.program_id(0)
    col_count = weight_ref.shape[1]
    tokens = normed_ref.shape[0]
    wide = normed_ref.shape[1]
    copies = [
        pltpu.make_async_copy(normed_hbm, normed_ref, sems.at[0]),
        pltpu.make_async_copy(og_hbm, og_ref, sems.at[1]),
        pltpu.make_async_copy(normed_t_hbm, normed_t_ref, sems.at[2]),
        pltpu.make_async_copy(og_t_hbm, og_t_ref, sems.at[3]),
    ]

    @pl.when(step == 0)
    def _():
        fill = pltpu.make_async_copy(residual_hbm, branch_ref, sems.at[5])
        fill.start()
        for copy in copies:
            copy.start()
        for copy in copies:
            copy.wait()
        back_ref[...] = jnp.zeros(back_ref.shape, f32)
        fill.wait()

    matrices = [[weight_ref.at[0, j, which] for j in range(col_count)] for which in range(3)]
    unit = Hidden(
        matrices, normed_ref, normed_t_ref, og_ref, og_t_ref, branch_ref, back_ref, hidden_ref,
        gate_ref, up_ref, lambda which, j: grad_ref.at[0, j, which],
    )
    unit.project(0, tokens // unit.block)
    unit.weights(0, wide // unit.span)

    @pl.when(step == pl.num_programs(0) - 1)
    def _():
        out = pltpu.make_async_copy(back_ref, back_hbm, sems.at[4])
        out.start()
        micro, model, rows = layer_ref.shape
        for m in range(micro):
            for k in range(model // shard_rows):
                source = slice(k * pad_rows, k * pad_rows + shard_rows)
                part = slice(k * shard_rows, (k + 1) * shard_rows)
                layer_ref[m, part, :] = branch_ref[source, m * rows : (m + 1) * rows].astype(bf16)
        out.wait()


def feed_forward(
    normed, normed_t, og, og_t, residual, weights, micro, model, shard_rows, pad_rows
):
    tokens, wide = normed.shape
    rows = tokens // micro
    steps, col_count = weights.shape[:2]
    width = col_count * tile
    anywhere = pl.BlockSpec(memory_space=pl.ANY)
    per_step = lambda: pl.BlockSpec((1,) + weights.shape[1:], lambda t: (t, 0, 0, 0, 0))
    return pl.pallas_call(
        functools.partial(feed_forward_kernel, shard_rows=shard_rows, pad_rows=pad_rows),
        grid=(steps,),
        in_specs=[anywhere] * 5 + [per_step()],
        out_specs=[
            pl.BlockSpec((micro, model, rows), lambda t: (0, 0, 0)),
            anywhere,
            per_step(),
        ],
        out_shape=[
            jax.ShapeDtypeStruct((micro, model, rows), bf16),
            jax.ShapeDtypeStruct((wide, tokens), f32),
            jax.ShapeDtypeStruct(weights.shape, bf16),
        ],
        scratch_shapes=[
            pltpu.VMEM((tokens, wide), bf16),
            pltpu.VMEM((wide, tokens), bf16),
            pltpu.VMEM((tokens, wide), bf16),
            pltpu.VMEM((wide, tokens), bf16),
            pltpu.VMEM((wide, tokens), f32),
            pltpu.VMEM((wide, tokens), f32),
            pltpu.VMEM((tokens, width), bf16),
            pltpu.VMEM((tokens, width), bf16),
            pltpu.VMEM((tokens, width), bf16),
            pltpu.SemaphoreType.DMA((6,)),
        ],
        compiler_params=pltpu.CompilerParams(vmem_limit_bytes=vmem_bytes),
        name="feed_forward",
    )(normed, normed_t, og, og_t, residual, weights)


def lane_fold(values):
    total = values[:, :tile]
    for q in range(1, values.shape[1] // tile):
        total = total + values[:, q * tile : (q + 1) * tile]
    return total


def padded_spans(start, stop, shard_rows, pad_rows):
    spans = []
    while start < stop:
        group, offset = divmod(start, shard_rows)
        size = min(stop - start, shard_rows - offset)
        spans.append((group * pad_rows + offset, size))
        start += size
    return spans


class Padded:
    def __init__(self, ref, shard_rows, pad_rows):
        self.ref, self.shard_rows, self.pad_rows = ref, shard_rows, pad_rows

    def read(self, start, stop):
        spans = padded_spans(start, stop, self.shard_rows, self.pad_rows)
        return jnp.concatenate([self.ref[at : at + size, :] for at, size in spans], axis=0)

    def write(self, start, stop, value):
        done = 0
        for at, size in padded_spans(start, stop, self.shard_rows, self.pad_rows):
            self.ref[at : at + size, :] = value[done : done + size]
            done += size


def attend_back(
    lens_ref,
    tok_ref,
    og_ref,
    wide_ref,
    back_ref,
    qkv_ref,
    attended_ref,
    log_ref,
    qkv_w_ref,
    out_w_ref,
    gains_ref,
    tok_grad_ref,
    tiles_ref,
    diag_ref,
    low_ref,
    grad_qkv_ref,
    fold_ref,
    add_out,
    add_qkv,
    before_heads,
    after_heads,
):
    model, rows = tok_ref.shape[1:]
    inner = attended_ref.shape[1]
    head_count = tiles_ref.shape[0]
    head_dim = inner // head_count
    blocks = rows // tile
    diag_count = 2 * blocks - 1
    size = model // 4
    quarters = [(k * size, (k + 1) * size) for k in range(4)]

    square = jnp.zeros((1, rows), f32)
    cross = jnp.zeros((1, rows), f32)
    for start, stop in quarters:
        x = wide_ref.read(start, stop)
        y = back_ref.read(start, stop)
        square = square + jnp.sum(x * x, axis=0, keepdims=True)
        cross = cross + jnp.sum(x * (y * gains_ref[start:stop, 1:2]), axis=0, keepdims=True)
    scale = lax.rsqrt(square / model + epsilon)
    pull = scale * scale * scale * (cross / model)
    for start, stop in quarters:
        x = wide_ref.read(start, stop)
        y = back_ref.read(start, stop)
        grad = og_ref[0, start:stop, :].astype(f32)
        grad = grad + scale * (y * gains_ref[start:stop, 1:2]) - x * pull
        wide_ref.write(start, stop, grad)
        low_ref[start:stop, :] = grad.astype(bf16)
        fold_ref[1, start:stop, :] += lane_fold(x * scale * y)
    for k, (start, stop) in enumerate(quarters):
        add_out(k, dot_nt(low_ref[start:stop, :], attended_ref[0]))
    grad_attended = dot_tn(out_w_ref[...], low_ref[...]).astype(bf16)
    grad_qkv_ref[0:inner, :] = grad_attended
    before_heads()

    same_doc = doc_labels(lens_ref, 0, rows) == doc_labels(lens_ref, 1, rows)

    def head(h, carry):
        base = pl.multiple_of(h * head_dim, head_dim)
        query_cols = qkv_ref[0, pl.ds(base, head_dim), :]
        key_cols = qkv_ref[0, pl.ds(inner + base, head_dim), :]
        value_cols = qkv_ref[0, pl.ds(2 * inner + base, head_dim), :]
        grad_cols = grad_qkv_ref[pl.ds(base, head_dim), :]
        scores = masked_scores(key_cols.T, query_cols, tiles_ref, h, same_doc, blocks)
        probs = jnp.exp(scores - log_ref[0, h, 0:1, :])
        grad_probs = dot_nn(value_cols.T, grad_cols)
        delta = jnp.sum(probs * grad_probs, axis=0, keepdims=True)
        grad_scores = (probs * (grad_probs - delta)).astype(bf16)
        grad_qkv_ref[pl.ds(2 * inner + base, head_dim), :] = dot_nt(
            grad_cols, probs.astype(bf16)
        ).astype(bf16)
        grad_qkv_ref[pl.ds(base, head_dim), :] = dot_nn(key_cols, grad_scores).astype(bf16)
        grad_qkv_ref[pl.ds(inner + base, head_dim), :] = dot_nt(query_cols, grad_scores).astype(
            bf16
        )
        wide = grad_scores.astype(f32)
        for d in range(diag_count):
            total = None
            for key_block in range(blocks):
                query_block = d - (blocks - 1) + key_block
                if 0 <= query_block < blocks:
                    piece = wide[
                        key_block * tile : (key_block + 1) * tile,
                        query_block * tile : (query_block + 1) * tile,
                    ]
                    total = piece if total is None else total + piece
            diag_ref[h, d] += total
        return carry

    lax.fori_loop(0, head_count, head, 0)
    after_heads()

    square = jnp.zeros((1, rows), f32)
    for start, stop in quarters:
        x = tok_ref[0, start:stop, :].astype(f32)
        square = square + jnp.sum(x * x, axis=0, keepdims=True)
    scale = lax.rsqrt(square / model + epsilon)
    cross = jnp.zeros((1, rows), f32)
    for k, (start, stop) in enumerate(quarters):
        x = tok_ref[0, start:stop, :].astype(f32)
        normed = (x * scale * gains_ref[start:stop, 0:1]).astype(bf16)
        add_qkv(k, dot_nt(normed, grad_qkv_ref[...]))
        y = dot_nn(qkv_w_ref[start:stop, :], grad_qkv_ref[...])
        back_ref.write(start, stop, y)
        cross = cross + jnp.sum(x * (y * gains_ref[start:stop, 0:1]), axis=0, keepdims=True)
        fold_ref[0, start:stop, :] += lane_fold(x * scale * y)
    pull = scale * scale * scale * (cross / model)
    for start, stop in quarters:
        x = tok_ref[0, start:stop, :].astype(f32)
        y = back_ref.read(start, stop)
        grad = wide_ref.read(start, stop) + scale * (y * gains_ref[start:stop, 0:1]) - x * pull
        tok_grad_ref[0, start:stop, :] = grad.astype(bf16)


def dot_exact(a, b, dims):
    return lax.dot_general(
        a, b, ((dims[:1], dims[1:]), ((), ())), preferred_element_type=f32, precision=highest
    )


def bucket_sums(diag_ref, bucket_ref, bucket_count, head_rows):
    head_count, diag_count = diag_ref.shape[:2]
    down = lax.broadcasted_iota(jnp.int32, (tile, tile), 0)
    across = lax.broadcasted_iota(jnp.int32, (tile, tile), 1)
    flip = (down + across == tile - 1).astype(f32)
    onehot = bucket_onehot(bucket_ref, bucket_count).astype(f32)
    rest = jnp.zeros((tile, tile), f32)
    lines = []
    for h in range(head_count):
        carry = jnp.zeros((1, tile), f32)
        pieces = []
        for d in range(diag_count):
            turned = dot_exact(flip, diag_ref[h, d], (1, 0))
            spread = pltpu.roll(
                jnp.concatenate([turned, rest], axis=1), 0, 1, stride=1, stride_axis=0
            )
            sums = jnp.sum(spread, axis=0, keepdims=True)
            pieces.append(sums[:, :tile] + carry)
            carry = sums[:, tile:]
        pieces.append(carry)
        lines.append(jnp.concatenate(pieces, axis=1))
    filler = jnp.zeros((head_rows - head_count, onehot.shape[1]), f32)
    return dot_exact(jnp.concatenate(lines + [filler], axis=0), onehot, (1, 1))


def gain_rows_of(fold_ref, start, stop):
    down = lax.broadcasted_iota(jnp.int32, (16, 2 * tile), 0)
    across = lax.broadcasted_iota(jnp.int32, (16, 2 * tile), 1)
    pick = (across // tile == down).astype(f32)
    both = jnp.concatenate([fold_ref[0, start:stop, :], fold_ref[1, start:stop, :]], axis=1)
    return dot_exact(pick, both, (1, 1))


def attention_backward_kernel(
    lens_ref,
    tok_ref,
    og_ref,
    residual_hbm,
    back_hbm,
    qkv_ref,
    attended_ref,
    log_ref,
    qkv_w_ref,
    out_w_ref,
    gains_ref,
    table_ref,
    bucket_ref,
    tok_grad_ref,
    qkv_grad_ref,
    out_grad_ref,
    table_grad_ref,
    gains_grad_ref,
    wide_ref,
    back_ref,
    tiles_ref,
    diag_ref,
    low_ref,
    grad_qkv_ref,
    fold_ref,
    sems,
    *,
    shard_rows,
    pad_rows,
):
    micro_index = pl.program_id(0)
    model, rows = tok_ref.shape[1:]
    size = model // 4
    start_load(residual_hbm, back_hbm, wide_ref, back_ref, sems, micro_index)

    @pl.when(micro_index == 0)
    def _():
        fill_bias_tiles([table_ref[...]], bucket_ref, tiles_ref)
        diag_ref[...] = jnp.zeros(diag_ref.shape, f32)
        fold_ref[...] = jnp.zeros(fold_ref.shape, f32)
        qkv_grad_ref[...] = jnp.zeros(qkv_grad_ref.shape, f32)
        out_grad_ref[...] = jnp.zeros(out_grad_ref.shape, f32)

    wait_load(residual_hbm, back_hbm, wide_ref, back_ref, sems, micro_index)

    def add_out(k, value):
        out_grad_ref[k * size : (k + 1) * size, :] += value

    def add_qkv(k, value):
        qkv_grad_ref[k * size : (k + 1) * size, :] += value

    nothing = lambda: None
    attend_back(
        lens_ref, tok_ref, og_ref, Padded(wide_ref, shard_rows, pad_rows),
        Padded(back_ref, shard_rows, pad_rows), qkv_ref, attended_ref, log_ref, qkv_w_ref,
        out_w_ref, gains_ref, tok_grad_ref, tiles_ref, diag_ref, low_ref, grad_qkv_ref, fold_ref,
        add_out, add_qkv, nothing, nothing,
    )

    @pl.when(micro_index == pl.num_programs(0) - 1)
    def _():
        gains_grad_ref[...] = gain_rows_of(fold_ref, 0, model)
        head_rows, bucket_count = table_grad_ref.shape
        table_grad_ref[...] = bucket_sums(diag_ref, bucket_ref, bucket_count, head_rows)


def load_copies(residual_hbm, back_hbm, wide_ref, back_ref, sems, m):
    rows = wide_ref.shape[1]
    cols = pl.ds(pl.multiple_of(m * rows, rows), rows)
    return [
        pltpu.make_async_copy(residual_hbm.at[:, cols], wide_ref, sems.at[0]),
        pltpu.make_async_copy(back_hbm.at[:, cols], back_ref, sems.at[1]),
    ]


def start_load(*args):
    for copy in load_copies(*args):
        copy.start()


def wait_load(*args):
    for copy in load_copies(*args):
        copy.wait()


def backward_inputs(lens, heads, inner, model, rows):
    whole = pl.BlockSpec(memory_space=pltpu.VMEM)
    anywhere = pl.BlockSpec(memory_space=pl.ANY)
    once = lambda shape: pl.BlockSpec(
        (1,) + shape, lambda m: (m,) + (0,) * len(shape), pipeline_mode=pl.Buffered(1)
    )
    return [
        pl.BlockSpec((1, 1, lens.shape[2]), lambda m: (m, 0, 0), memory_space=pltpu.SMEM),
        once((model, rows)),
        once((model, rows)),
        anywhere,
        anywhere,
        once((3 * inner, rows)),
        once((inner, rows)),
        once((heads, 8, rows)),
        whole,
        whole,
        whole,
        whole,
        whole,
    ]


def backward_scratch(heads, inner, model, rows, wide):
    diag_count = 2 * (rows // tile) - 1
    return [
        pltpu.VMEM((wide, rows), f32),
        pltpu.VMEM((wide, rows), f32),
        pltpu.VMEM((heads, diag_count, tile, tile), bf16),
        pltpu.VMEM((heads, diag_count, tile, tile), f32),
        pltpu.VMEM((model, rows), bf16),
        pltpu.VMEM((3 * inner, rows), bf16),
        pltpu.VMEM((2, model, tile), f32),
        pltpu.SemaphoreType.DMA((2,)),
    ]


def attention_backward(
    lens, tok, og, residual, back, qkv, attended, log_total, qkv_w, out_w, gains, table, bucket,
    shard_rows, pad_rows,
):
    micro, model, rows = tok.shape
    inner = out_w.shape[1]
    heads = log_total.shape[1]
    wide = back.shape[0]
    whole = pl.BlockSpec(memory_space=pltpu.VMEM)
    return pl.pallas_call(
        functools.partial(attention_backward_kernel, shard_rows=shard_rows, pad_rows=pad_rows),
        grid=(micro,),
        in_specs=backward_inputs(lens, heads, inner, model, rows),
        out_specs=[pl.BlockSpec((1, model, rows), lambda m: (m, 0, 0))] + [whole] * 4,
        out_shape=[
            jax.ShapeDtypeStruct((micro, model, rows), bf16),
            jax.ShapeDtypeStruct((model, 3 * inner), f32),
            jax.ShapeDtypeStruct((model, inner), f32),
            jax.ShapeDtypeStruct((table.shape[0], table.shape[1]), f32),
            jax.ShapeDtypeStruct((16, model), f32),
        ],
        scratch_shapes=backward_scratch(heads, inner, model, rows, wide),
        compiler_params=pltpu.CompilerParams(vmem_limit_bytes=vmem_bytes),
        name="attention_backward",
    )(lens, tok, og, residual, back, qkv, attended, log_total, qkv_w, out_w, gains, table, bucket)


class Place:
    def __init__(self, row_count):
        self.row_count = row_count
        self.y = lax.axis_index("dp")
        self.z = lax.axis_index("row")
        col = lax.axis_index("col")
        self.x = col // 2
        self.core = col % 2
        self.near_x = self.x + (1 - self.core) * (1 - 2 * self.x)
        self.near_y = self.y + self.core * (1 - 2 * self.y)
        self.far_x = self.x + self.core * (1 - 2 * self.x)
        self.far_y = self.y + (1 - self.core) * (1 - 2 * self.y)

    def at(self, x, y, z, core):
        return (y, z, 2 * x + core)

    def near(self):
        return self.at(self.near_x, self.near_y, self.z, self.core)

    def far(self):
        return self.at(self.far_x, self.far_y, self.z, self.core)

    def partner(self):
        return self.at(self.x, self.y, self.z, 1 - self.core)

    def beside_y(self):
        return self.at(self.x, 1 - self.y, self.z, self.core)

    def beside_x(self):
        return self.at(1 - self.x, self.y, self.z, self.core)

    def along(self, step):
        return self.at(self.x, self.y, lax.rem(self.z + step, self.row_count), self.core)

    def greet(self, across=False):
        barrier = pltpu.get_barrier_semaphore()
        others = [self.near(), self.far(), self.partner()]
        for step in range(1, self.row_count):
            others.append(self.along(step))
            if across:
                z = lax.rem(self.z + step, self.row_count)
                others.append(self.at(1 - self.x, self.y, z, self.core))
        for other in others:
            pl.semaphore_signal(barrier, inc=1, device_id=other, device_id_type=MESH)
        pl.semaphore_wait(barrier, len(others))


def send(source, target, send_sem, recv_sem, device):
    return pltpu.make_async_remote_copy(
        src_ref=source,
        dst_ref=target,
        send_sem=send_sem,
        recv_sem=recv_sem,
        device_id=device,
        device_id_type=MESH,
    )


def gather_semaphores(steps, row_count):
    dma = pltpu.SemaphoreType.DMA
    return [
        dma((steps,)),
        dma((2, steps, row_count - 1)),
        dma((2, steps, 3)),
        dma((2, steps, 4)),
    ]


class Gather:
    def __init__(self, place, shard_ref, full_ref, sems, base=0):
        self.place, self.shard, self.full, self.base = place, shard_ref, full_ref, base
        self.local, self.line, self.cross, self.pair = sems
        self.pad_rows = shard_ref.shape[2]
        self.unit_rows = self.pad_rows * place.row_count

    def unit(self, t, x, y, core):
        rows = pl.ds(pl.multiple_of(y * self.unit_rows, self.unit_rows), self.unit_rows)
        return self.full.at[t - self.base, 2 * x + core, :, rows, :]

    def own(self, t):
        p = self.place
        index = p.y * p.row_count + p.z
        rows = pl.ds(pl.multiple_of(index * self.pad_rows, self.pad_rows), self.pad_rows)
        return self.full.at[t - self.base, 2 * p.x + p.core, :, rows, :]

    def copy_local(self, t):
        return pltpu.make_async_copy(self.shard.at[t], self.own(t), self.local.at[t])

    def copy_line(self, t, step):
        return send(
            self.shard.at[t],
            self.own(t),
            self.line.at[0, t, step - 1],
            self.line.at[1, t, step - 1],
            self.place.along(step),
        )

    def copy_cross(self, t, which):
        p = self.place
        x, y = ((p.x, p.y), (p.x, p.y), (p.near_x, p.near_y))[which]
        unit = self.unit(t, x, y, p.core)
        device = p.near() if which == 0 else p.far()
        return send(unit, unit, self.cross.at[0, t, which], self.cross.at[1, t, which], device)

    def copy_pair(self, t, which):
        p = self.place
        x, y = (
            (p.x, p.y),
            (p.near_x, p.near_y),
            (p.far_x, p.far_y),
            (1 - p.x, 1 - p.y),
        )[which]
        unit = self.unit(t, x, y, p.core)
        return send(
            unit, unit, self.pair.at[0, t, which], self.pair.at[1, t, which], p.partner()
        )

    def begin(self, t):
        self.copy_local(t).start()
        for step in range(1, self.place.row_count):
            self.copy_line(t, step).start()

    def spread(self, t):
        self.copy_local(t).wait()
        for step in range(1, self.place.row_count):
            self.copy_line(t, step).wait_recv()
        self.copy_cross(t, 0).start()
        self.copy_cross(t, 1).start()
        self.copy_pair(t, 0).start()

    def relay(self, t):
        self.copy_cross(t, 0).wait_recv()
        self.copy_cross(t, 2).start()
        self.copy_pair(t, 1).start()
        self.copy_cross(t, 1).wait_recv()
        self.copy_pair(t, 2).start()

    def settle(self, t):
        self.copy_cross(t, 2).wait_recv()
        self.copy_pair(t, 3).start()

    def finish(self, t):
        for which in range(4):
            self.copy_pair(t, which).wait_recv()

    def drain(self, t):
        for step in range(1, self.place.row_count):
            self.copy_line(t, step).wait_send()
        for which in range(3):
            self.copy_cross(t, which).wait_send()
        for which in range(4):
            self.copy_pair(t, which).wait_send()


class Share:
    def __init__(self, place, pairs, sems):
        self.place, self.pairs, self.sems = place, pairs, sems

    def rows(self, ref, core):
        half = ref.shape[0] // 2
        return pl.ds(pl.multiple_of(core * half, half), half)

    def copy_local(self, i):
        own, full = self.pairs[i]
        return pltpu.make_async_copy(own, full.at[self.place.y], self.sems.at[0, i, 0])

    def copy_over(self, i):
        own, full = self.pairs[i]
        p = self.place
        rows = self.rows(own, p.core)
        return send(
            own.at[rows, :],
            full.at[p.y, rows, :],
            self.sems.at[0, i, 1],
            self.sems.at[1, i, 1],
            p.beside_y(),
        )

    def copy_pair(self, i):
        own, full = self.pairs[i]
        p = self.place
        part = full.at[1 - p.y, self.rows(own, p.core), :]
        return send(part, part, self.sems.at[0, i, 2], self.sems.at[1, i, 2], p.partner())

    def begin(self):
        for i in range(len(self.pairs)):
            self.copy_over(i).start()
        for i in range(len(self.pairs)):
            self.copy_local(i).start()

    def relay(self):
        for i in range(len(self.pairs)):
            self.copy_over(i).wait_recv()
            self.copy_pair(i).start()

    def finish(self):
        for i in range(len(self.pairs)):
            self.copy_local(i).wait()
            self.copy_pair(i).wait_recv()

    def drain(self):
        for i in range(len(self.pairs)):
            self.copy_over(i).wait_send()
            self.copy_pair(i).wait_send()


def add_into(into, other):
    into[...] = into[...] + other[...]


def tables_of(small_ref, table_rows, bucket_part):
    return [small_ref[y, 16 : 16 + table_rows, 0:bucket_part] for y in range(2)]


def fused_forward_kernel(
    lens_ref, tok_ref, og_ref, bucket_ref, shard_ref, qkv_own, out_own, small_own,
    normed_ref, normed_t_ref, og_pad_ref, og_pad_t_ref, qkv_ref, attended_ref, log_ref,
    residual_ref, full_ref, qkv_full, out_full, small_full, gains_full,
    tiles_ref, scaled_ref, gains_ref, qkv_w_ref, out_w_ref, small_ref,
    local, line, cross, pair, share_sems, keep_sems,
    *, row_count, shard_rows, pad_rows, table_rows, bucket_part,
):
    micro_index = pl.program_id(0)
    early = full_ref.shape[0]
    part = qkv_own.shape[0]
    place = Place(row_count)
    gather = Gather(place, shard_ref, full_ref, (local, line, cross, pair))
    share = Share(
        place,
        [(small_own, small_ref), (qkv_own, qkv_w_ref), (out_own, out_w_ref)],
        share_sems,
    )
    keeps = [
        pltpu.make_async_copy(source, target, keep_sems.at[i])
        for i, (source, target) in enumerate(
            (
                (qkv_w_ref, qkv_full),
                (out_w_ref, out_full),
                (small_ref, small_full),
                (gains_ref, gains_full),
            )
        )
    ]

    @pl.when(micro_index == 0)
    def _():
        place.greet()
        share.begin()
        for t in range(early):
            gather.begin(t)

    pad_cotangent(og_ref, og_pad_ref, og_pad_t_ref, shard_rows, pad_rows)

    @pl.when(micro_index == 0)
    def _():
        gather.spread(0)
        share.relay()
        for t in range(1, early):
            gather.spread(t)
        share.finish()
        for y in range(2):
            turned = small_ref[y, 0:16, :].astype(f32).T
            gains_ref[y * part : (y + 1) * part, :] = turned[:part, :]
        for keep in keeps:
            keep.start()
        fill_bias_tiles(tables_of(small_ref, table_rows, bucket_part), bucket_ref, tiles_ref)

    def between():
        @pl.when(micro_index == 0)
        def _():
            gather.relay(0)

        @pl.when(micro_index == 1)
        def _():
            gather.settle(0)

    attend(
        lens_ref, tok_ref, qkv_w_ref, out_w_ref, gains_ref, normed_ref, normed_t_ref, qkv_ref,
        attended_ref, log_ref, residual_ref, tiles_ref, scaled_ref, shard_rows, pad_rows, between,
    )

    @pl.when(micro_index == 0)
    def _():
        for t in range(1, early):
            gather.relay(t)

    @pl.when(micro_index == 1)
    def _():
        for t in range(1, early):
            gather.settle(t)
        share.drain()
        for keep in keeps:
            keep.wait()
        for t in range(early):
            gather.finish(t)
            gather.drain(t)


def fused_forward(
    lens, tok, og, bucket, shard, qkv_w, out_w, small, heads, early, shard_rows, pad_rows,
    row_count, col_count, bucket_part,
):
    micro, model, rows = tok.shape
    inner = out_w.shape[1]
    steps, kinds = shard.shape[:2]
    wide = model // shard_rows * pad_rows
    anywhere = pl.BlockSpec(memory_space=pl.ANY)
    whole = pl.BlockSpec(memory_space=pltpu.VMEM)
    once = lambda shape: pl.BlockSpec((1,) + shape, lambda m: (m,) + (0,) * len(shape))
    double = lambda a: jax.ShapeDtypeStruct((2,) + a.shape, a.dtype)
    out_specs, out_shape = forward_outputs(micro, heads, inner, model, rows, wide)
    dma = pltpu.SemaphoreType.DMA
    return pl.pallas_call(
        functools.partial(
            fused_forward_kernel, row_count=row_count, shard_rows=shard_rows, pad_rows=pad_rows,
            table_rows=16, bucket_part=bucket_part,
        ),
        grid=(micro,),
        in_specs=[
            pl.BlockSpec((1, 1, lens.shape[2]), lambda m: (m, 0, 0), memory_space=pltpu.SMEM),
            once((model, rows)),
            once((model, rows)),
            whole,
        ]
        + [anywhere] * 4,
        out_specs=out_specs + [anywhere] * 5,
        out_shape=out_shape
        + [
            jax.ShapeDtypeStruct((early, col_count, kinds, wide, tile), bf16),
            double(qkv_w),
            double(out_w),
            double(small),
            jax.ShapeDtypeStruct((model, 16), f32),
        ],
        scratch_shapes=[
            pltpu.VMEM((heads, 2 * (rows // tile) - 1, tile, tile), bf16),
            pltpu.VMEM((model, rows), f32),
            pltpu.VMEM((model, 16), f32),
            pltpu.VMEM((2,) + qkv_w.shape, bf16),
            pltpu.VMEM((2,) + out_w.shape, bf16),
            pltpu.VMEM((2,) + small.shape, bf16),
        ]
        + gather_semaphores(steps, row_count)
        + [dma((2, 3, 3)), dma((4,))],
        compiler_params=pltpu.CompilerParams(
            collective_id=0, has_side_effects=True, vmem_limit_bytes=vmem_bytes
        ),
        name="fused_forward",
    )(lens, tok, og, bucket, shard, qkv_w, out_w, small)


def fused_hidden_kernel(
    normed_hbm, normed_t_hbm, og_hbm, og_t_hbm, residual_hbm, first_ref, shard_ref,
    layer_hbm, back_hbm, sums_hbm, rest_ref, landed_hbm,
    normed_ref, normed_t_ref, og_ref, og_t_ref, branch_ref, back_ref, hidden_ref, gate_ref, up_ref,
    weight_ref, grad_ref, other_ref, layer_ref,
    local, line, cross, pair, load_sems, weight_sems, store_sems, swap_sems, far_sems,
    credit,
    *, row_count, shard_rows, pad_rows,
):
    t = pl.program_id(0)
    steps, col_count = shard_ref.shape[0], weight_ref.shape[1]
    early = first_ref.shape[0]
    tokens, wide = normed_ref.shape
    place = Place(row_count)
    slot = lax.rem(t, 2)
    gather = Gather(place, shard_ref, rest_ref, (local, line, cross, pair), early)
    reduce = Reduce(place, sums_hbm, landed_hbm, far_sems)
    ahead = landed_hbm.shape[0]

    def load_early(q):
        s = lax.rem(q, 2)
        return pltpu.make_async_copy(first_ref.at[q], weight_ref.at[s], weight_sems.at[s])

    def load_late(q):
        s = lax.rem(q, 2)
        return pltpu.make_async_copy(rest_ref.at[q - early], weight_ref.at[s], weight_sems.at[s])

    def swap(q):
        s = lax.rem(q, 2)
        return send(
            grad_ref.at[s, :, 1 - place.core], other_ref.at[s], swap_sems.at[0, q],
            swap_sems.at[1, q], place.partner(),
        )

    def store(q):
        s = lax.rem(q, 2)
        return pltpu.make_async_copy(
            grad_ref.at[s, :, place.core], sums_hbm.at[q], store_sems.at[s]
        )

    def fold(q):
        s = lax.rem(q, 2)
        swap(q).wait_recv()
        for x in range(col_count // 2):
            for kind in range(3):
                add_into(grad_ref.at[s, x, place.core, kind], other_ref.at[s, x, kind])
        store(q).start()

        @pl.when(q < steps - 2)
        def _():
            pl.semaphore_signal(credit, 1, device_id=place.partner(), device_id_type=MESH)

    def late(q):
        return (q >= early) & (q < steps)

    @pl.when(t == 0)
    def _():
        loads = [
            pltpu.make_async_copy(source, target, load_sems.at[i])
            for i, (source, target) in enumerate(
                (
                    (normed_hbm, normed_ref),
                    (og_hbm, og_ref),
                    (normed_t_hbm, normed_t_ref),
                    (og_t_hbm, og_t_ref),
                    (residual_hbm, branch_ref),
                )
            )
        ]
        load_early(0).start()
        for load in loads:
            load.start()
        place.greet()
        for q in range(early, steps):
            gather.begin(q)
        back_ref[...] = jnp.zeros(back_ref.shape, f32)
        for load in loads:
            load.wait()
        for q in range(early, 4):
            gather.spread(q)

    @pl.when(t < early)
    def _():
        load_early(t).wait()

    @pl.when(t >= early)
    def _():
        load_late(t).wait()

    weights_now = weight_ref.at[slot]
    matrices = [[weights_now.at[j, which] for j in range(col_count)] for which in range(3)]
    unit = Hidden(
        matrices, normed_ref, normed_t_ref, og_ref, og_t_ref, branch_ref, back_ref, hidden_ref,
        gate_ref, up_ref, lambda which, j: grad_ref.at[slot, j // 2, j % 2, which],
    )
    unit.project(0, tokens // unit.block)

    @pl.when(t >= 1)
    def _():
        fold(t - 1)

    @pl.when(t >= 2)
    def _():
        swap(t - 2).wait_send()
        store(t - 2).wait()

    def send_far(step, chunks):
        @pl.when(t == step)
        def _():
            for q in chunks:
                reduce.begin(q)

    send_far(steps - 2, [2])
    send_far(steps - 1, [4])

    spans = wide // unit.span
    unit.weights(0, spans - 1)

    @pl.when(late(t + 2))
    def _():
        gather.relay(t + 2)

    @pl.when(late(t + 4))
    def _():
        gather.spread(t + 4)

    @pl.when(late(t + 1))
    def _():
        gather.settle(t + 1)

    @pl.when(t + 1 < early)
    def _():
        load_early(t + 1).start()

    send_far(steps - 3, [0, 1])
    send_far(steps - 2, [3])

    unit.weights(spans - 1, spans)

    @pl.when(late(t + 1))
    def _():
        gather.finish(t + 1)
        load_late(t + 1).start()

    @pl.when(t >= 2)
    def _():
        pl.semaphore_wait(credit, 1)

    swap(t).start()

    @pl.when(t == steps - 1)
    def _():
        out = pltpu.make_async_copy(back_ref, back_hbm, load_sems.at[0])
        out.start()
        rows = layer_ref.shape[1]
        for m in range(tokens // rows):
            for k in range(wide // pad_rows):
                source = slice(k * pad_rows, k * pad_rows + shard_rows)
                part = slice(k * shard_rows, (k + 1) * shard_rows)
                layer_ref[part, :] = branch_ref[source, m * rows : (m + 1) * rows].astype(bf16)
            layer_out = pltpu.make_async_copy(layer_ref, layer_hbm.at[m], load_sems.at[1])
            layer_out.start()
            layer_out.wait()
        fold(t)
        swap(t - 1).wait_send()
        swap(t).wait_send()
        store(t - 1).wait()
        store(t).wait()
        out.wait()
        for q in range(early, steps):
            gather.drain(q)
        for q in range(ahead):
            for which in range(2):
                reduce.copy_far(q, which).wait()


def fused_hidden(
    normed, normed_t, og, og_t, residual, first, shard, micro, model, shard_rows, pad_rows,
    row_count, ahead,
):
    tokens, wide = normed.shape
    rows = tokens // micro
    steps, kinds = shard.shape[:2]
    early, col_count = first.shape[:2]
    x_count = col_count // 2
    width = col_count * tile
    anywhere = pl.BlockSpec(memory_space=pl.ANY)
    dma = pltpu.SemaphoreType.DMA
    return pl.pallas_call(
        functools.partial(
            fused_hidden_kernel, row_count=row_count, shard_rows=shard_rows, pad_rows=pad_rows
        ),
        grid=(steps,),
        in_specs=[anywhere] * 7,
        out_specs=[anywhere] * 5,
        out_shape=[
            jax.ShapeDtypeStruct((micro, model, rows), bf16),
            jax.ShapeDtypeStruct((wide, tokens), f32),
            jax.ShapeDtypeStruct((steps, x_count, kinds, wide, tile), bf16),
            jax.ShapeDtypeStruct((steps - early,) + first.shape[1:], bf16),
            jax.ShapeDtypeStruct((ahead, 2, kinds, pad_rows * row_count, tile), bf16),
        ],
        scratch_shapes=[
            pltpu.VMEM((tokens, wide), bf16),
            pltpu.VMEM((wide, tokens), bf16),
            pltpu.VMEM((tokens, wide), bf16),
            pltpu.VMEM((wide, tokens), bf16),
            pltpu.VMEM((wide, tokens), f32),
            pltpu.VMEM((wide, tokens), f32),
            pltpu.VMEM((tokens, width), bf16),
            pltpu.VMEM((tokens, width), bf16),
            pltpu.VMEM((tokens, width), bf16),
            pltpu.VMEM((2, col_count, kinds, wide, tile), bf16),
            pltpu.VMEM((2, x_count, 2, kinds, wide, tile), bf16),
            pltpu.VMEM((2, x_count, kinds, wide, tile), bf16),
            pltpu.VMEM((model, rows), bf16),
        ]
        + gather_semaphores(steps, row_count)
        + [
            dma((5,)),
            dma((2,)),
            dma((2,)),
            dma((2, steps)),
            dma((2, ahead, 2)),
            pltpu.SemaphoreType.REGULAR,
        ],
        compiler_params=pltpu.CompilerParams(
            collective_id=1, has_side_effects=True, vmem_limit_bytes=vmem_bytes
        ),
        name="fused_hidden",
    )(normed, normed_t, og, og_t, residual, first, shard)


class Reduce:
    slots = 2

    def __init__(
        self, place, source, second, cross, landed=None, landed_sems=None, stage=None, third=None,
        fourth=None, load=None, line=None,
    ):
        self.place, self.source, self.second, self.cross = place, source, second, cross
        self.landed, self.landed_sems, self.stage = landed, landed_sems, stage
        self.third, self.fourth, self.load, self.line = third, fourth, load, line
        self.unit_rows = second.shape[3]
        self.pad_rows = self.unit_rows // place.row_count
        self.ahead = 0 if landed is None else landed.shape[0]

    def unit(self, t, x, y):
        rows = pl.ds(pl.multiple_of(y * self.unit_rows, self.unit_rows), self.unit_rows)
        return self.source.at[t, x, :, rows, :]

    def shard(self, row):
        return pl.ds(pl.multiple_of(row * self.pad_rows, self.pad_rows), self.pad_rows)

    def copy_own(self, t, which):
        p = self.place
        slot = t % self.slots
        x, y = ((p.x, p.y), (p.near_x, p.near_y))[which]
        return pltpu.make_async_copy(
            self.unit(t, x, y), self.stage.at[slot, which], self.load.at[slot, which]
        )

    def copy_far(self, t, which):
        p = self.place
        x, y = ((p.far_x, p.far_y), (1 - p.x, 1 - p.y))[which]
        return send(
            self.unit(t, x, y), self.second.at[t, which], self.cross.at[0, t, which],
            self.cross.at[1, t, which], p.far(),
        )

    def copy_near(self, t):
        return send(
            self.second.at[t, 1], self.third.at[t], self.cross.at[0, t, 2],
            self.cross.at[1, t, 2], self.place.near(),
        )

    def copy_line(self, t, step):
        p = self.place
        rows = self.shard(lax.rem(p.z + step, p.row_count))
        return send(
            self.second.at[t, 0, :, rows, :], self.fourth.at[t, step - 1],
            self.line.at[0, t, step - 1], self.line.at[1, t, step - 1], p.along(step),
        )

    def copy_landed(self, t):
        return pltpu.make_async_copy(
            self.landed.at[t], self.second.at[t], self.landed_sems.at[t]
        )

    def load_own(self, t):
        for which in range(2):
            self.copy_own(t, which).start()

    def begin(self, t):
        self.copy_far(t, 1).start()
        self.copy_far(t, 0).start()

    def fold_far(self, t):
        self.copy_own(t, 1).wait()
        if t < self.ahead:
            self.copy_landed(t).wait()
        else:
            self.copy_far(t, 1).wait_recv()
        slot = t % self.slots
        for kind in range(3):
            add_into(self.second.at[t, 1, kind], self.stage.at[slot, 1, kind])
        self.copy_near(t).start()
        self.copy_own(t, 0).wait()
        if t >= self.ahead:
            self.copy_far(t, 0).wait_recv()
        for kind in range(3):
            add_into(self.second.at[t, 0, kind], self.stage.at[slot, 0, kind])

    def fold_near(self, t):
        self.copy_near(t).wait_recv()
        for kind in range(3):
            add_into(self.second.at[t, 0, kind], self.third.at[t, kind])
        for step in range(1, self.place.row_count):
            self.copy_line(t, step).start()

    def total(self, t, kind):
        total = self.second[t, 0, kind, self.shard(self.place.z), :].astype(f32)
        for step in range(1, self.place.row_count):
            total = total + self.fourth[t, step - 1, kind].astype(f32)
        return total

    def wait_line(self, t):
        for step in range(1, self.place.row_count):
            self.copy_line(t, step).wait_recv()

    def drain(self, t):
        if t >= self.ahead:
            for which in range(2):
                self.copy_far(t, which).wait_send()
        self.copy_near(t).wait_send()
        for step in range(1, self.place.row_count):
            self.copy_line(t, step).wait_send()


class Dense:
    def __init__(self, place, source, first, second, third, piece, out, sems):
        self.place, self.source = place, source
        self.first, self.second, self.third, self.piece = first, second, third, piece
        self.out, self.sems = out, sems
        self.half = second.shape[0]
        self.piece_rows = piece.shape[0]
        self.offsets = [
            (dx, dz) for dx in range(2) for dz in range(place.row_count) if (dx, dz) != (0, 0)
        ]

    def rows(self, start, size):
        return pl.ds(pl.multiple_of(start, 16), size)

    def sem(self, i):
        return self.sems.at[0, i], self.sems.at[1, i]

    def half_rows(self, core):
        return self.rows(core * self.half, self.half)

    def piece_at(self, dx, dz):
        p = self.place
        x = p.x + dx * (1 - 2 * p.x)
        z = lax.rem(p.z + dz, p.row_count)
        start = p.core * self.half + (x * p.row_count + z) * self.piece_rows
        return self.rows(start, self.piece_rows)

    def other(self, dx, dz):
        p = self.place
        x = p.x + dx * (1 - 2 * p.x)
        return p.at(x, p.y, lax.rem(p.z + dz, p.row_count), p.core)

    def copy_pair(self):
        p = self.place
        return send(
            self.source.at[:, self.half_rows(1 - p.core), :], self.first, *self.sem(0), p.partner()
        )

    def copy_y(self):
        p = self.place
        part = self.source.at[1 - p.y, self.half_rows(p.core), :]
        return send(part, self.second, *self.sem(1), p.beside_y())

    def copy_piece(self, i):
        part = self.source.at[self.place.y, self.piece_at(*self.offsets[i]), :]
        return send(part, self.third.at[i], *self.sem(3 + i), self.other(*self.offsets[i]))

    def keep_piece(self):
        return pltpu.make_async_copy(
            self.piece, self.out.at[self.piece_at(0, 0), :], self.sems.at[0, 2]
        )

    def back_piece(self, i):
        part = self.out.at[self.piece_at(0, 0), :]
        index = 3 + len(self.offsets) + i
        return send(self.piece, part, *self.sem(index), self.other(*self.offsets[i]))

    def back_pair(self):
        p = self.place
        part = self.out.at[self.half_rows(p.core), :]
        return send(part, part, *self.sem(3 + 2 * len(self.offsets)), p.partner())

    def begin(self):
        self.copy_pair().start()

    def fold_pair(self):
        p = self.place
        self.copy_pair().wait_recv()
        rows = self.half_rows(p.core)
        add_into(self.source.at[1 - p.y, rows, :], self.first.at[1 - p.y])
        self.copy_y().start()
        add_into(self.source.at[p.y, rows, :], self.first.at[p.y])

    def fold_y(self):
        p = self.place
        self.copy_y().wait_recv()
        add_into(self.source.at[p.y, self.half_rows(p.core), :], self.second)
        for i in range(len(self.offsets)):
            self.copy_piece(i).start()

    def fold_pieces(self):
        for i in range(len(self.offsets)):
            self.copy_piece(i).wait_recv()
        total = self.source[self.place.y, self.piece_at(0, 0), :].astype(f32)
        for i in range(len(self.offsets)):
            total = total + self.third[i].astype(f32)
        self.piece[...] = total.astype(bf16)
        self.keep_piece().start()
        for i in range(len(self.offsets)):
            self.back_piece(i).start()

    def return_pair(self):
        self.keep_piece().wait()
        for i in range(len(self.offsets)):
            self.back_piece(i).wait_recv()
        self.back_pair().start()

    def finish(self):
        self.back_pair().wait_recv()
        self.copy_pair().wait_send()
        self.copy_y().wait_send()
        self.back_pair().wait_send()
        for i in range(len(self.offsets)):
            self.copy_piece(i).wait_send()
            self.back_piece(i).wait_send()


def fused_backward_kernel(
    lens_ref, tok_ref, og_ref, residual_hbm, back_hbm, qkv_ref, attended_ref, log_ref, qkv_w_ref,
    out_w_ref, gains_ref, small_ref, bucket_ref, source_ref, landed_ref,
    tok_grad_ref, inner_ref, outer_ref, dense_out,
    wide_ref, back_ref, tiles_ref, diag_ref, low_ref, grad_qkv_ref, fold_ref, load_sems,
    stage, second, third, fourth,
    dense_ref, dense_first, dense_second, dense_third, dense_piece,
    load, cross, line, landed_sems, dense_sems,
    *, row_count, shard_rows, pad_rows, bucket_part,
):
    micro_index = pl.program_id(0)
    model, rows = tok_ref.shape[1:]
    inner = attended_ref.shape[1]
    part = model // 2
    size = model // 4
    steps = source_ref.shape[0]
    place = Place(row_count)
    reduce = Reduce(
        place, source_ref, second, cross, landed_ref, landed_sems, stage, third, fourth, load, line
    )
    dense = Dense(
        place, dense_ref, dense_first, dense_second, dense_third, dense_piece, dense_out,
        dense_sems,
    )

    def finish_chunk(t):
        reduce.wait_line(t)
        lanes = slice(t * tile, (t + 1) * tile)
        for kind in range(2):
            inner_ref[kind, :, lanes] = reduce.total(t, kind)[:shard_rows]
        outer_ref[:, lanes] = reduce.total(t, 2)[:shard_rows]

    def group(n):
        if n < steps:
            reduce.fold_far(n)
            if n + reduce.slots < steps:
                reduce.load_own(n + reduce.slots)
        if 0 <= n - 1 < steps:
            reduce.fold_near(n - 1)
        if 0 <= n - 2 < steps:
            finish_chunk(n - 2)

    start_load(residual_hbm, back_hbm, wide_ref, back_ref, load_sems, micro_index)

    @pl.when(micro_index == 0)
    def _():
        for t in range(reduce.slots):
            reduce.load_own(t)
        for t in range(reduce.ahead):
            reduce.copy_landed(t).start()
        place.greet(True)
        group(0)
        fill_bias_tiles(tables_of(small_ref, 16, bucket_part), bucket_ref, tiles_ref)
        diag_ref[...] = jnp.zeros(diag_ref.shape, f32)
        fold_ref[...] = jnp.zeros(fold_ref.shape, f32)
        dense_ref[...] = jnp.zeros(dense_ref.shape, bf16)

    wait_load(residual_hbm, back_hbm, wide_ref, back_ref, load_sems, micro_index)

    def add(k, start, value):
        at = (k // 2, slice((k % 2) * size, (k % 2 + 1) * size), slice(start, start + value.shape[1]))
        dense_ref[at] = (dense_ref[at].astype(f32) + value).astype(bf16)

    def before_heads():
        @pl.when(micro_index == 0)
        def _():
            group(1)
            for t in range(reduce.ahead, steps):
                reduce.begin(t)

        @pl.when(micro_index == 1)
        def _():
            group(3)

    def after_heads():
        @pl.when(micro_index == 0)
        def _():
            group(2)

        @pl.when(micro_index == 1)
        def _():
            group(4)

    attend_back(
        lens_ref, tok_ref, og_ref, Padded(wide_ref, shard_rows, pad_rows),
        Padded(back_ref, shard_rows, pad_rows), qkv_ref, attended_ref, log_ref, qkv_w_ref,
        out_w_ref, gains_ref, tok_grad_ref, tiles_ref, diag_ref, low_ref, grad_qkv_ref, fold_ref,
        lambda k, value: add(k, 3 * inner, value), lambda k, value: add(k, 0, value),
        before_heads, after_heads,
    )

    @pl.when(micro_index == 1)
    def _():
        half = bucket_part
        sums = bucket_sums(diag_ref, bucket_ref, 2 * half, 16).astype(bf16)
        for y in range(2):
            gains = gain_rows_of(fold_ref, y * part, (y + 1) * part)
            dense_ref[y, part : part + 16, 0:part] = gains.astype(bf16)
            dense_ref[y, part + 16 : part + 32, 0:half] = sums[:, y * half : (y + 1) * half]
        dense.begin()
        group(5)
        dense.fold_pair()
        group(6)
        dense.fold_y()
        group(7)
        dense.fold_pieces()
        for n in range(8, steps + 2):
            group(n)
        dense.return_pair()
        dense.finish()
        for t in range(steps):
            reduce.drain(t)


def fused_backward(
    lens, tok, og, residual, back, qkv, attended, log_total, qkv_w, out_w, gains, small, bucket,
    source, landed, dense_rows, shard_rows, pad_rows, row_count, bucket_part,
):
    micro, model, rows = tok.shape
    inner = out_w.shape[1]
    heads = log_total.shape[1]
    steps, x_count, kinds, wide, _ = source.shape
    unit_rows = pad_rows * row_count
    slots = Reduce.slots
    width = 4 * inner
    half = dense_rows // 2
    piece_rows = half // (2 * row_count)
    hidden = steps * tile
    anywhere = pl.BlockSpec(memory_space=pl.ANY)
    inside = pl.BlockSpec(memory_space=pltpu.VMEM)
    dma = pltpu.SemaphoreType.DMA
    return pl.pallas_call(
        functools.partial(
            fused_backward_kernel, row_count=row_count, shard_rows=shard_rows, pad_rows=pad_rows,
            bucket_part=bucket_part,
        ),
        grid=(micro,),
        in_specs=backward_inputs(lens, heads, inner, model, rows) + [anywhere] * 2,
        out_specs=[
            pl.BlockSpec(
                (1, model, rows), lambda m: (m, 0, 0), pipeline_mode=pl.Buffered(1)
            ),
            inside,
            inside,
            anywhere,
        ],
        out_shape=[
            jax.ShapeDtypeStruct((micro, model, rows), bf16),
            jax.ShapeDtypeStruct((2, shard_rows, hidden), f32),
            jax.ShapeDtypeStruct((shard_rows, hidden), f32),
            jax.ShapeDtypeStruct((dense_rows, width), bf16),
        ],
        scratch_shapes=backward_scratch(heads, inner, model, rows, wide)
        + [
            pltpu.VMEM((slots, 2, kinds, unit_rows, tile), bf16),
            pltpu.VMEM((steps, 2, kinds, unit_rows, tile), bf16),
            pltpu.VMEM((steps, kinds, unit_rows, tile), bf16),
            pltpu.VMEM((steps, row_count - 1, kinds, pad_rows, tile), bf16),
            pltpu.VMEM((2, dense_rows, width), bf16),
            pltpu.VMEM((2, half, width), bf16),
            pltpu.VMEM((half, width), bf16),
            pltpu.VMEM((2 * row_count - 1, piece_rows, width), bf16),
            pltpu.VMEM((piece_rows, width), bf16),
            dma((slots, 2)),
            dma((2, steps, 3)),
            dma((2, steps, row_count - 1)),
            dma((landed.shape[0],)),
            dma((2, 4 + 2 * (2 * row_count - 1))),
        ],
        compiler_params=pltpu.CompilerParams(
            collective_id=2, has_side_effects=True, vmem_limit_bytes=vmem_bytes
        ),
        name="fused_backward",
    )(
        lens, tok, og, residual, back, qkv, attended, log_total, qkv_w, out_w, gains, small,
        bucket, source, landed,
    )


def round_up(value, multiple):
    return -(-value // multiple) * multiple


def shards(
    tokens,
    out_grad,
    lengths,
    offset_bucket,
    qkv_weight,
    out_weight,
    bias_table,
    norm_gains,
    inner_weight,
    outer_weight,
):
    dp_count, row_count, col_count = (lax.axis_size(a) for a in ("dp", "row", "col"))
    shard_count = dp_count * row_count
    micro, rows, model = tokens.shape
    shard_rows = inner_weight.shape[1]
    hidden = inner_weight.shape[2]
    steps = hidden // tile
    heads = bias_table.shape[1]
    bucket_part = bias_table.shape[0]
    bucket_count = bucket_part * dp_count
    inner = out_weight.shape[0]
    part = qkv_weight.shape[0]
    head_rows = 16
    direct = (
        dp_count == 2 and col_count == 4 and part % 32 == 0 and shard_rows % 8 == 0 and steps >= 7
        and micro == 2
    )

    group_rows = shard_rows if direct else model // 2
    pad_rows = round_up(group_rows, 16 if direct else 256)

    tok_t = jnp.transpose(tokens, (0, 2, 1))
    og_t = jnp.transpose(out_grad, (0, 2, 1))
    out_part = out_weight.T
    small_width = round_up(max(part, bucket_part), tile)
    gain_rows = 16
    small = jnp.concatenate(
        [
            jnp.pad(norm_gains, ((0, gain_rows - 2), (0, small_width - part))),
            jnp.pad(bias_table.T, ((0, head_rows - heads), (0, small_width - bucket_part))),
        ],
        axis=0,
    )
    bucket = jnp.pad(offset_bucket[::-1], (0, 1), constant_values=-1)[None, :]
    packed = jnp.stack([inner_weight[0], inner_weight[1], outer_weight.T])
    if direct:
        packed = jnp.pad(packed, ((0, 0), (0, pad_rows - shard_rows), (0, 0)))
        packed = packed.reshape(3, pad_rows, steps, tile).transpose(2, 0, 1, 3)
        (
            normed, normed_t, og_pad, og_pad_t, qkv, attended, log_total, residual, first,
            qkv_full, out_full, small_full, gains,
        ) = fused_forward(
            lengths, tok_t, og_t, bucket, packed, qkv_weight, out_part, small, heads,
            2, group_rows, pad_rows, row_count, col_count, bucket_part,
        )
    else:
        packed = packed.reshape(3, shard_rows, steps, tile).transpose(2, 0, 1, 3)
        weights = lax.all_gather(packed, ("dp", "row"), axis=2, tiled=True)
        weights = jnp.moveaxis(lax.all_gather(weights, "col", axis=0), 0, 1)
        weights = weights.reshape(steps, col_count, 3, 2, group_rows, tile)
        weights = jnp.pad(weights, ((0, 0),) * 4 + ((0, pad_rows - group_rows), (0, 0)))
        weights = weights.reshape(steps, col_count, 3, 2 * pad_rows, tile)
        qkv_full, out_full, small_full = (
            lax.all_gather(a, "dp", axis=0) for a in (qkv_weight, out_part, small)
        )
    qkv_full = qkv_full.reshape(1, model, 3 * inner)
    out_full = out_full.reshape(1, model, inner)
    if direct:
        layer_t, back, sums, _, landed = fused_hidden(
            normed, normed_t, og_pad, og_pad_t, residual, first, packed, micro, model, group_rows,
            pad_rows, row_count, 5,
        )
    else:
        gains = small_full[:, :2, :part].transpose(0, 2, 1).reshape(model, 2).astype(f32)
        table = small_full[:, gain_rows : gain_rows + head_rows, :bucket_part]
        table = table.transpose(1, 0, 2).reshape(head_rows, bucket_count)
        normed, normed_t, og_pad, og_pad_t, qkv, attended, log_total, residual = attention_forward(
            lengths, tok_t, og_t, qkv_full, out_full, gains, table, bucket, heads, group_rows,
            pad_rows,
        )
        layer_t, back, weight_grads = feed_forward(
            normed, normed_t, og_pad, og_pad_t, residual, weights, micro, model, group_rows,
            pad_rows,
        )
    qkv_full, out_full = qkv_full[0], out_full[0]
    backward = (
        lengths, tok_t, og_t, residual, back, qkv, attended, log_total, qkv_full, out_full, gains,
    )
    dense_rows = round_up(part + 32, 64 * row_count)
    if direct:
        tok_grad_t, inner_grad, outer_grad, total = fused_backward(
            *backward, small_full, bucket, sums, landed, dense_rows, group_rows, pad_rows, row_count,
            bucket_part,
        )
    else:
        tok_grad_t, qkv_grad, out_grads, table_grad, gains_grad = attention_backward(
            *backward, table, bucket, group_rows, pad_rows
        )
        width = 4 * inner
        table_part = table_grad.reshape(head_rows, dp_count, bucket_part).transpose(1, 0, 2)
        gains_part = gains_grad.reshape(16, dp_count, part).transpose(1, 0, 2)
        rest = dense_rows - part - 32
        dense = jnp.concatenate([qkv_grad, out_grads], axis=1).reshape(dp_count, part, width)
        dense = jnp.concatenate(
            [
                dense,
                jnp.pad(gains_part, ((0, 0), (0, 0), (0, width - part))),
                jnp.pad(table_part, ((0, 0), (0, rest), (0, width - bucket_part))),
            ],
            axis=1,
        ).astype(bf16)
        grads = weight_grads.reshape(steps, col_count, 3, 2, pad_rows, tile)
        grads = grads[:, :, :, :, :group_rows].reshape(steps, col_count, 3, model, tile)
        grads = jnp.moveaxis(grads, 1, 0)
        grads = lax.psum_scatter(grads, "col", scatter_dimension=0)
        grads = lax.psum_scatter(grads, ("dp", "row"), scatter_dimension=2, tiled=True)
        grads = grads.transpose(1, 2, 0, 3).reshape(3, shard_rows, hidden)
        inner_grad, outer_grad = grads[:2].astype(f32), grads[2].astype(f32)
        total = lax.psum_scatter(dense, "dp", scatter_dimension=0)
        total = lax.psum(total, ("row", "col"))
    total = total.astype(f32)
    return (
        jnp.transpose(layer_t, (0, 2, 1)),
        jnp.transpose(tok_grad_t, (0, 2, 1)),
        total[:part, : 3 * inner],
        total[:part, 3 * inner :].T,
        total[part + 16 : part + 16 + heads, :bucket_part].T,
        total[part : part + 2, :part],
        inner_grad,
        outer_grad.T,
    )


def solution(mesh):
    return jax.shard_map(
        shards,
        mesh=mesh,
        in_specs=(
            P(None, ("dp", "row", "col"), None),
            P(None, ("dp", "row", "col"), None),
            P(None, ("dp", "row", "col"), None),
            P(),
            P("dp", None),
            P(None, "dp"),
            P("dp", None),
            P(None, "dp"),
            P(None, ("dp", "row"), "col"),
            P("col", ("dp", "row")),
        ),
        out_specs=(
            P(None, ("dp", "row", "col"), None),
            P(None, ("dp", "row", "col"), None),
            P("dp", None),
            P(None, "dp"),
            P("dp", None),
            P(None, "dp"),
            P(None, ("dp", "row"), "col"),
            P("col", ("dp", "row")),
        ),
        check_vma=False,
    )
```

time: 1560 us -> 479 us (0.31)
  waiting for transfers between devices: 762 us -> 0 us
  Pallas kernels: 0 us -> 457 us
  local copies, waits for them, and re-layouts: 372 us -> 15.1 us
  matrix products: 291 us -> 0 us
  other arithmetic: 61.7 us -> 4.39 us
  blocking collectives: 43 us -> 0 us
    pallas_call x0 -> x3, Pallas kernels: none -> 457 us  [the longest x1 203 us: fused_hidden(): pl.pallas_call(functools.partial(fused_hidden_kernel, row_count=row_count...]
    reduce_scatter x7 -> x0, waiting for transfers between devices: 441 us -> none  [the longest x1 183 us: shards(): lax.psum_scatter(inner_acc, ('dp', 'row'), scatter_dimension=1, tiled=True)]
    dot_general x45 -> x0, matrix products: 291 us -> none  [the longest x2 40.5 us: shards(): jnp.einsum('td,fd->tf', grad_rows, outer_back, preferred_element_type=jnp...]
    all_gather x8 -> x0, waiting for transfers between devices: 197 us -> none  [the longest x2 89.4 us: shards(): gathered = lax.all_gather(normed_two, 'col', axis=0, tiled=True)]
    unnamed x190 -> x16, local copies, waits for them, and re-layouts: 146 us -> 7.94 us
    rev x3 -> x0, local copies, waits for them, and re-layouts: 126 us -> none  [the longest x2 77.3 us: diagonal_sums(): flipped = jnp.pad(score_grid[:, :, ::-1], ((0, 0), (0, 0), (0, row_count)))]
    unnamed x22 -> x0, waiting for transfers between devices: 104 us -> none
    reshape x7 -> x0, local copies, waits for them, and re-layouts: 42.7 us -> none  [the longest x2 28.6 us: diagonal_sums(): skewed = skewed.reshape(head_count, row_count, 2 * row_count - 1)]
  transfers between devices with their start and end apart: 19 -> 0, of which waited for: 13 -> 0; matrix products, arithmetic and copies ran while one was open for 38% -> 0% of each run, Pallas kernels for 0% -> 0%
where the time goes in v1:
time: 479 us; the launch traced here: 478 us
  Pallas kernels  457 us (95%)
  local copies, waits for them, and re-layouts  15.1 us (3%)
    pallas_call x1, Pallas kernels, fused_hidden(): pl.pallas_call(functools.partial(fused_hidden_kernel, row_count=row_count...  203 us
    pallas_call x1, Pallas kernels, fused_backward(): pl.pallas_call(functools.partial(fused_backward_kernel, row_count=row_cou...  175 us
    pallas_call x1, Pallas kernels, fused_forward(): pl.pallas_call(functools.partial(fused_forward_kernel, row_count=row_coun...  79.5 us

profile of v1, /device:TPU:0, one launch (start us, length us, event | category | flops | bytes accessed | tf_op | source)
XLA Modules:
  0.0 477.6 jit_solution(9395956741789387030)
XLA Ops:
  0.6 0.8 reverse
  1.4 0.1 slice.25
  1.5 0.6 pad.16
  2.1 1.3 fusion.6.small_own
  3.4 2.4 bitcast_bitcast_fusion.shard_ref
  5.8 79.5 %fused_forward.1 = (bf16[1024,1536]{1,0:T(8,128)(2,1)}, bf16[1536,1024]{1,0:T(8,128)(2,1)}, bf16[1024,1536]{1,0:T(8,128)(2,1)}, bf16[1536,1024]{1,0:T(8,128)(2,1...) custom-call(s32[2,1,2]{2,1,0:T(1,128)} %lens_ref.3, ...), custom_call_target="tpu_custom_call" | custom-call | tf_op jit(solution)/shard_map/fused_forward/pallas_call | solution.py:1088
  85.3 202.5 %fused_hidden.1 = (bf16[2,1472,512]{2,1,0:T(8,128)(2,1)}, f32[1536,1024]{1,0:T(8,128)}, bf16[7,2,3,1536,128]{4,3,2,1,0:T(8,128)(2,1)}, bf16[5,4,3,1536,128]{4,3,2,1,0:T(8,128)(2,1)}, bf16[5,2,3,768,128]{4,3,2,1,0:T(8,128)(2,1)}) custom-call(bf16[1024,1536]{1,0:T(8,128)(2,1)} %get-tuple-element.29.normed_hbm, ...), custom_call_target="tpu_custom_call" | custom-call | tf_op jit(solution)/shard_map/fused_hidden/pallas_call | solution.py:1315
  287.9 175.4 %fused_backward.1 = (bf16[2,1472,512]{2,1,0:T(8,128)(2,1)}, f32[2,184,896]{2,1,0:T(8,128)}, f32[184,896]{1,0:T(8,128)}, bf16[768,1536]{1,0:T(8,128)(2,1)}) custom-call(s32[2,1,2]{2,1,0:T(1,128)} %lens_ref.3, bf16[2,1472,512]{2,1,0:T(8,128)(2,1)} %bitcast.26, bf16[2,1472,512]{2,1,0:T(8,128)(2,1)} %bitcast.28, f32[1536,1024]{1,0:T(8,128)} %get-tuple-element.33.residual_hbm, ...), custom_call_target="tpu_custom_call" | custom-call | tf_op jit(solution)/shard_map/fused_backward/pallas_call | solution.py:1704
  463.3 1.3 slice.22
  464.6 0.0 copy-start
  464.6 3.6 slice.19
  468.1 0.0 copy-done
  468.1 0.0 copy-start.1
  468.1 0.6 convert_element_type.9
  468.8 0.6 slice_bitcast_fusion.1
  469.4 1.1 slice_bitcast_fusion
  470.5 0.0 copy-done.1
  470.5 1.6 copy.25
  472.1 1.3 copy-done.2
  473.4 1.6 copy.26
  475.0 0.6 copy-done.3
  475.7 1.1 copy.27
  476.7 0.0 copy-done.4
  476.7 0.8 copy.28
  (3 shorter events, 0.0 us)
Async XLA Ops:
  464.6 3.6 copy-start
  468.1 2.3 copy-start.1
  470.5 2.9 copy-start.2
  473.4 2.3 copy-start.3
  473.4 3.3 copy-start.4

commit v2 on v1

--- a/solution.py
+++ b/solution.py
@@ -1237,7 +1237,6 @@
                 reduce.begin(q)
 
     send_far(steps - 2, [2])
-    send_far(steps - 1, [4])
 
     spans = wide // unit.span
     unit.weights(0, spans - 1)
@@ -1400,12 +1399,14 @@
             self.cross.at[1, t, 2], self.place.near(),
         )
 
-    def copy_line(self, t, step):
+    def copy_line(self, t, i):
         p = self.place
-        rows = self.shard(lax.rem(p.z + step, p.row_count))
+        beside = p.z + 1 - 2 * lax.rem(p.z, 2)
+        shard = (beside, lax.rem(beside + 2, 4), lax.rem(p.z + 2, 4))[i]
+        to = beside if i < 2 else shard
         return send(
-            self.second.at[t, 0, :, rows, :], self.fourth.at[t, step - 1],
-            self.line.at[0, t, step - 1], self.line.at[1, t, step - 1], p.along(step),
+            self.second.at[t, 0, :, self.shard(shard), :], self.fourth.at[t, i],
+            self.line.at[0, t, i], self.line.at[1, t, i], p.at(p.x, p.y, to, p.core),
         )
 
     def copy_landed(self, t):
@@ -1441,38 +1442,46 @@
         self.copy_near(t).wait_recv()
         for kind in range(3):
             add_into(self.second.at[t, 0, kind], self.third.at[t, kind])
-        for step in range(1, self.place.row_count):
-            self.copy_line(t, step).start()
+        self.copy_line(t, 0).start()
+        self.copy_line(t, 1).start()
+
+    def fold_line(self, t):
+        p = self.place
+        for i in range(2):
+            self.copy_line(t, i).wait_recv()
+        for i, shard in ((1, lax.rem(p.z + 2, 4)), (0, p.z)):
+            for kind in range(3):
+                add_into(
+                    self.second.at[t, 0, kind, self.shard(shard), :], self.fourth.at[t, i, kind]
+                )
+            if i == 1:
+                self.copy_line(t, 2).start()
 
     def total(self, t, kind):
-        total = self.second[t, 0, kind, self.shard(self.place.z), :].astype(f32)
-        for step in range(1, self.place.row_count):
-            total = total + self.fourth[t, step - 1, kind].astype(f32)
-        return total
+        own = self.second[t, 0, kind, self.shard(self.place.z), :].astype(f32)
+        return own + self.fourth[t, 2, kind].astype(f32)
 
     def wait_line(self, t):
-        for step in range(1, self.place.row_count):
-            self.copy_line(t, step).wait_recv()
+        self.copy_line(t, 2).wait_recv()
 
     def drain(self, t):
         if t >= self.ahead:
             for which in range(2):
                 self.copy_far(t, which).wait_send()
         self.copy_near(t).wait_send()
-        for step in range(1, self.place.row_count):
-            self.copy_line(t, step).wait_send()
+        for i in range(3):
+            self.copy_line(t, i).wait_send()
 
 
 class Dense:
-    def __init__(self, place, source, first, second, third, piece, out, sems):
+    def __init__(self, place, source, first, second, third, fourth, piece, out, sems):
         self.place, self.source = place, source
-        self.first, self.second, self.third, self.piece = first, second, third, piece
-        self.out, self.sems = out, sems
-        self.half = second.shape[0]
-        self.piece_rows = piece.shape[0]
-        self.offsets = [
-            (dx, dz) for dx in range(2) for dz in range(place.row_count) if (dx, dz) != (0, 0)
-        ]
+        self.first, self.second, self.third, self.fourth = first, second, third, fourth
+        self.piece, self.out, self.sems = piece, out, sems
+        self.half, self.quarter, self.piece_rows = (
+            second.shape[0], third.shape[0], piece.shape[0],
+        )
+        self.others = range(1, place.row_count)
 
     def rows(self, start, size):
         return pl.ds(pl.multiple_of(start, 16), size)
@@ -1483,17 +1492,14 @@
     def half_rows(self, core):
         return self.rows(core * self.half, self.half)
 
-    def piece_at(self, dx, dz):
+    def quarter_rows(self, x):
+        return self.rows(self.place.core * self.half + x * self.quarter, self.quarter)
+
+    def piece_at(self, step):
         p = self.place
-        x = p.x + dx * (1 - 2 * p.x)
-        z = lax.rem(p.z + dz, p.row_count)
-        start = p.core * self.half + (x * p.row_count + z) * self.piece_rows
+        z = lax.rem(p.z + step, p.row_count)
+        start = p.core * self.half + p.x * self.quarter + z * self.piece_rows
         return self.rows(start, self.piece_rows)
-
-    def other(self, dx, dz):
-        p = self.place
-        x = p.x + dx * (1 - 2 * p.x)
-        return p.at(x, p.y, lax.rem(p.z + dz, p.row_count), p.core)
 
     def copy_pair(self):
         p = self.place
@@ -1506,24 +1512,32 @@
         part = self.source.at[1 - p.y, self.half_rows(p.core), :]
         return send(part, self.second, *self.sem(1), p.beside_y())
 
-    def copy_piece(self, i):
-        part = self.source.at[self.place.y, self.piece_at(*self.offsets[i]), :]
-        return send(part, self.third.at[i], *self.sem(3 + i), self.other(*self.offsets[i]))
+    def copy_x(self):
+        p = self.place
+        part = self.source.at[p.y, self.quarter_rows(1 - p.x), :]
+        return send(part, self.third, *self.sem(2), p.beside_x())
+
+    def copy_piece(self, step):
+        part = self.source.at[self.place.y, self.piece_at(step), :]
+        return send(part, self.fourth.at[step - 1], *self.sem(5 + step), self.place.along(step))
 
     def keep_piece(self):
         return pltpu.make_async_copy(
-            self.piece, self.out.at[self.piece_at(0, 0), :], self.sems.at[0, 2]
-        )
-
-    def back_piece(self, i):
-        part = self.out.at[self.piece_at(0, 0), :]
-        index = 3 + len(self.offsets) + i
-        return send(self.piece, part, *self.sem(index), self.other(*self.offsets[i]))
+            self.piece, self.out.at[self.piece_at(0), :], self.sems.at[0, 3]
+        )
+
+    def back_piece(self, step):
+        index = 5 + self.place.row_count + step
+        part = self.out.at[self.piece_at(0), :]
+        return send(self.piece, part, *self.sem(index), self.place.along(step))
+
+    def back_x(self):
+        part = self.out.at[self.quarter_rows(self.place.x), :]
+        return send(part, part, *self.sem(4), self.place.beside_x())
 
     def back_pair(self):
-        p = self.place
-        part = self.out.at[self.half_rows(p.core), :]
-        return send(part, part, *self.sem(3 + 2 * len(self.offsets)), p.partner())
+        part = self.out.at[self.half_rows(self.place.core), :]
+        return send(part, part, *self.sem(5), self.place.partner())
 
     def begin(self):
         self.copy_pair().start()
@@ -1540,34 +1554,51 @@
         p = self.place
         self.copy_y().wait_recv()
         add_into(self.source.at[p.y, self.half_rows(p.core), :], self.second)
-        for i in range(len(self.offsets)):
-            self.copy_piece(i).start()
+        self.copy_x().start()
+
+    def fold_x(self):
+        p = self.place
+        self.copy_x().wait_recv()
+        add_into(self.source.at[p.y, self.quarter_rows(p.x), :], self.third)
+        for step in self.others:
+            self.copy_piece(step).start()
 
     def fold_pieces(self):
-        for i in range(len(self.offsets)):
-            self.copy_piece(i).wait_recv()
-        total = self.source[self.place.y, self.piece_at(0, 0), :].astype(f32)
-        for i in range(len(self.offsets)):
-            total = total + self.third[i].astype(f32)
+        for step in self.others:
+            self.copy_piece(step).wait_recv()
+        total = self.source[self.place.y, self.piece_at(0), :].astype(f32)
+        for step in self.others:
+            total = total + self.fourth[step - 1].astype(f32)
         self.piece[...] = total.astype(bf16)
         self.keep_piece().start()
-        for i in range(len(self.offsets)):
-            self.back_piece(i).start()
+        for step in self.others:
+            self.back_piece(step).start()
+
+    def return_x(self):
+        self.keep_piece().wait()
+        for step in self.others:
+            self.back_piece(step).wait_recv()
+        self.back_x().start()
 
     def return_pair(self):
-        self.keep_piece().wait()
-        for i in range(len(self.offsets)):
-            self.back_piece(i).wait_recv()
+        self.back_x().wait_recv()
         self.back_pair().start()
 
     def finish(self):
         self.back_pair().wait_recv()
-        self.copy_pair().wait_send()
-        self.copy_y().wait_send()
-        self.back_pair().wait_send()
-        for i in range(len(self.offsets)):
-            self.copy_piece(i).wait_send()
-            self.back_piece(i).wait_send()
+        for copy in (
+            self.copy_pair(), self.copy_y(), self.copy_x(), self.back_x(), self.back_pair(),
+        ):
+            copy.wait_send()
+        for step in self.others:
+            self.copy_piece(step).wait_send()
+            self.back_piece(step).wait_send()
+
+
+def dense_lanes(inner):
+    tiles = 3 * inner // tile
+    cut = (tiles + 1) // 2 * tile
+    return [(3 * inner, inner), (0, cut), (cut, 3 * inner - cut)]
 
 
 def fused_backward_kernel(
@@ -1576,24 +1607,29 @@
     tok_grad_ref, inner_ref, outer_ref, dense_out,
     wide_ref, back_ref, tiles_ref, diag_ref, low_ref, grad_qkv_ref, fold_ref, load_sems,
     stage, second, third, fourth,
-    dense_ref, dense_first, dense_second, dense_third, dense_piece,
-    load, cross, line, landed_sems, dense_sems,
-    *, row_count, shard_rows, pad_rows, bucket_part,
+    dense_ref, load, cross, line, landed_sems, *dense_scratch, row_count, shard_rows, pad_rows, bucket_part,
 ):
     micro_index = pl.program_id(0)
     model, rows = tok_ref.shape[1:]
     inner = attended_ref.shape[1]
     part = model // 2
-    size = model // 4
+    quarter = model // 4
     steps = source_ref.shape[0]
     place = Place(row_count)
     reduce = Reduce(
         place, source_ref, second, cross, landed_ref, landed_sems, stage, third, fourth, load, line
     )
-    dense = Dense(
-        place, dense_ref, dense_first, dense_second, dense_third, dense_piece, dense_out,
-        dense_sems,
-    )
+    streams = []
+    for i, (start, size) in enumerate(dense_lanes(inner)):
+        first, swapped, across, pieces, piece, sems = dense_scratch[6 * i : 6 * i + 6]
+        lanes = pl.ds(start, size)
+        streams.append(
+            Dense(
+                place, dense_ref.at[:, :, lanes], first, swapped, across, pieces, piece,
+                dense_out.at[:, lanes], sems,
+            )
+        )
+    out, left, right = streams
 
     def finish_chunk(t):
         reduce.wait_line(t)
@@ -1610,7 +1646,9 @@
         if 0 <= n - 1 < steps:
             reduce.fold_near(n - 1)
         if 0 <= n - 2 < steps:
-            finish_chunk(n - 2)
+            reduce.fold_line(n - 2)
+        if 0 <= n - 3 < steps:
+            finish_chunk(n - 3)
 
     start_load(residual_hbm, back_hbm, wide_ref, back_ref, load_sems, micro_index)
 
@@ -1620,7 +1658,7 @@
             reduce.load_own(t)
         for t in range(reduce.ahead):
             reduce.copy_landed(t).start()
-        place.greet(True)
+        place.greet()
         group(0)
         fill_bias_tiles(tables_of(small_ref, 16, bucket_part), bucket_ref, tiles_ref)
         diag_ref[...] = jnp.zeros(diag_ref.shape, f32)
@@ -1630,7 +1668,7 @@
     wait_load(residual_hbm, back_hbm, wide_ref, back_ref, load_sems, micro_index)
 
     def add(k, start, value):
-        at = (k // 2, slice((k % 2) * size, (k % 2 + 1) * size), slice(start, start + value.shape[1]))
+        at = (k // 2, slice((k % 2) * quarter, (k % 2 + 1) * quarter), slice(start, start + value.shape[1]))
         dense_ref[at] = (dense_ref[at].astype(f32) + value).astype(bf16)
 
     def before_heads():
@@ -1642,6 +1680,7 @@
 
         @pl.when(micro_index == 1)
         def _():
+            out.begin()
             group(3)
 
     def after_heads():
@@ -1651,6 +1690,7 @@
 
         @pl.when(micro_index == 1)
         def _():
+            out.fold_pair()
             group(4)
 
     attend_back(
@@ -1669,17 +1709,33 @@
             gains = gain_rows_of(fold_ref, y * part, (y + 1) * part)
             dense_ref[y, part : part + 16, 0:part] = gains.astype(bf16)
             dense_ref[y, part + 16 : part + 32, 0:half] = sums[:, y * half : (y + 1) * half]
-        dense.begin()
+        left.begin()
+        right.begin()
+        out.fold_y()
         group(5)
-        dense.fold_pair()
+        left.fold_pair()
+        right.fold_pair()
+        out.fold_x()
         group(6)
-        dense.fold_y()
+        left.fold_y()
+        right.fold_y()
+        out.fold_pieces()
         group(7)
-        dense.fold_pieces()
-        for n in range(8, steps + 2):
+        left.fold_x()
+        right.fold_x()
+        out.return_x()
+        group(8)
+        left.fold_pieces()
+        right.fold_pieces()
+        out.return_pair()
+        for n in range(9, steps + 3):
             group(n)
-        dense.return_pair()
-        dense.finish()
+        left.return_x()
+        right.return_x()
+        left.return_pair()
+        right.return_pair()
+        for stream in streams:
+            stream.finish()
         for t in range(steps):
             reduce.drain(t)
 
@@ -1701,6 +1757,16 @@
     anywhere = pl.BlockSpec(memory_space=pl.ANY)
     inside = pl.BlockSpec(memory_space=pltpu.VMEM)
     dma = pltpu.SemaphoreType.DMA
+    dense_buffers = []
+    for _, size in dense_lanes(inner):
+        dense_buffers += [
+            pltpu.VMEM((2, half, size), bf16),
+            pltpu.VMEM((half, size), bf16),
+            pltpu.VMEM((half // 2, size), bf16),
+            pltpu.VMEM((row_count - 1, piece_rows, size), bf16),
+            pltpu.VMEM((piece_rows, size), bf16),
+            dma((2, 6 + 2 * row_count)),
+        ]
     return pl.pallas_call(
         functools.partial(
             fused_backward_kernel, row_count=row_count, shard_rows=shard_rows, pad_rows=pad_rows,
@@ -1729,16 +1795,12 @@
             pltpu.VMEM((steps, kinds, unit_rows, tile), bf16),
             pltpu.VMEM((steps, row_count - 1, kinds, pad_rows, tile), bf16),
             pltpu.VMEM((2, dense_rows, width), bf16),
-            pltpu.VMEM((2, half, width), bf16),
-            pltpu.VMEM((half, width), bf16),
-            pltpu.VMEM((2 * row_count - 1, piece_rows, width), bf16),
-            pltpu.VMEM((piece_rows, width), bf16),
             dma((slots, 2)),
             dma((2, steps, 3)),
             dma((2, steps, row_count - 1)),
             dma((landed.shape[0],)),
-            dma((2, 4 + 2 * (2 * row_count - 1))),
-        ],
+        ]
+        + dense_buffers,
         compiler_params=pltpu.CompilerParams(
             collective_id=2, has_side_effects=True, vmem_limit_bytes=vmem_bytes
         ),
@@ -1779,7 +1841,7 @@
     head_rows = 16
     direct = (
         dp_count == 2 and col_count == 4 and part % 32 == 0 and shard_rows % 8 == 0 and steps >= 7
-        and micro == 2
+        and micro == 2 and inner % tile == 0 and row_count == 4
     )
 
     group_rows = shard_rows if direct else model // 2
@@ -1824,7 +1886,7 @@
     if direct:
         layer_t, back, sums, _, landed = fused_hidden(
             normed, normed_t, og_pad, og_pad_t, residual, first, packed, micro, model, group_rows,
-            pad_rows, row_count, 5,
+            pad_rows, row_count, 4,
         )
     else:
         gains = small_full[:, :2, :part].transpose(0, 2, 1).reshape(model, 2).astype(f32)

time: 479 us -> 454 us (0.948)
  Pallas kernels: 457 us -> 434 us
    pallas_call x1, Pallas kernels: 203 us -> 190 us  [fused_hidden(): pl.pallas_call(functools.partial(fused_hidden_kernel, row_count=row_count...]
    pallas_call x1, Pallas kernels: 175 us -> 164 us  [fused_backward(): pl.pallas_call(functools.partial(fused_backward_kernel, row_count=row_cou...]
where the time goes in v2:
time: 454 us
  Pallas kernels  434 us (96%)
  local copies, waits for them, and re-layouts  15.1 us (3%)
    pallas_call x1, Pallas kernels, fused_hidden(): pl.pallas_call(functools.partial(fused_hidden_kernel, row_count=row_count...  190 us
    pallas_call x1, Pallas kernels, fused_backward(): pl.pallas_call(functools.partial(fused_backward_kernel, row_count=row_cou...  164 us
    pallas_call x1, Pallas kernels, fused_forward(): pl.pallas_call(functools.partial(fused_forward_kernel, row_count=row_coun...  79.6 us

profile of v2, /device:TPU:0, one launch (start us, length us, event | category | flops | bytes accessed | tf_op | source)
XLA Modules:
  0.0 453.7 jit_solution(1838256777577468743)
XLA Ops:
  0.6 0.8 reverse
  1.4 0.1 slice.25
  1.5 0.6 pad.16
  2.1 1.3 fusion.6.small_own
  3.4 2.4 bitcast_bitcast_fusion.shard_ref
  5.8 79.6 %fused_forward.1 = (bf16[1024,1536]{1,0:T(8,128)(2,1)}, bf16[1536,1024]{1,0:T(8,128)(2,1)}, bf16[1024,1536]{1,0:T(8,128)(2,1)}, bf16[1536,1024]{1,0:T(8,128)(2,1...) custom-call(s32[2,1,2]{2,1,0:T(1,128)} %lens_ref.3, ...), custom_call_target="tpu_custom_call" | custom-call | tf_op jit(solution)/shard_map/fused_forward/pallas_call | solution.py:1088
  85.4 189.8 %fused_hidden.1 = (bf16[2,1472,512]{2,1,0:T(8,128)(2,1)}, f32[1536,1024]{1,0:T(8,128)}, bf16[7,2,3,1536,128]{4,3,2,1,0:T(8,128)(2,1)}, bf16[5,4,3,1536,128]{4,3,2,1,0:T(8,128)(2,1)}, bf16[4,2,3,768,128]{4,3,2,1,0:T(8,128)(2,1)}) custom-call(bf16[1024,1536]{1,0:T(8,128)(2,1)} %get-tuple-element.29.normed_hbm, ...), custom_call_target="tpu_custom_call" | custom-call | tf_op jit(solution)/shard_map/fused_hidden/pallas_call | solution.py:1314
  275.2 164.2 %fused_backward.1 = (bf16[2,1472,512]{2,1,0:T(8,128)(2,1)}, f32[2,184,896]{2,1,0:T(8,128)}, f32[184,896]{1,0:T(8,128)}, bf16[768,1536]{1,0:T(8,128)(2,1)}) custom-call(s32[2,1,2]{2,1,0:T(1,128)} %lens_ref.3, bf16[2,1472,512]{2,1,0:T(8,128)(2,1)} %bitcast.26, bf16[2,1472,512]{2,1,0:T(8,128)(2,1)} %bitcast.28, f32[1536,1024]{1,0:T(8,128)} %get-tuple-element.33.residual_hbm, ...), custom_call_target="tpu_custom_call" | custom-call | tf_op jit(solution)/shard_map/fused_backward/pallas_call | solution.py:1770
  439.4 1.3 slice.22
  440.7 0.0 copy-start
  440.7 3.6 slice.19
  444.3 0.0 copy-done
  444.3 0.0 copy-start.1
  444.3 0.6 convert_element_type.9
  444.9 0.6 slice_bitcast_fusion.1
  445.5 1.1 slice_bitcast_fusion
  446.6 0.0 copy-done.1
  446.6 1.6 copy.25
  448.3 1.3 copy-done.2
  449.6 1.6 copy.26
  451.2 0.6 copy-done.3
  451.8 1.1 copy.27
  452.9 0.0 copy-done.4
  452.9 0.8 copy.28
  (3 shorter events, 0.0 us)
Async XLA Ops:
  440.7 3.6 copy-start
  444.3 2.3 copy-start.1
  446.6 2.9 copy-start.2
  449.6 2.3 copy-start.3
  449.6 3.3 copy-start.4
